TPU v7x, 512 devices: a whole 4x4x16 slice. The times are simulated.
512 devices in a mesh: sx: 32 (over z, y_hi), sy: 16 (over x, y_lo, core).
Axes of the slice: x: 4, y: 4 (y_hi: 2, y_lo: 2; y = y_hi * 2 + y_lo), z: 16, core: 2. Of those that a mesh axis runs over, the one named last changes fastest.
Arguments:
- volume: bfloat16 [4, 256, 128, 128], P(None, 'sx', 'sy'), may hold values from -6 to 6
- w_first: bfloat16 [16, 4, 3, 3, 3], replicated, may hold values from -0.625 to 0.625
- w_second: bfloat16 [32, 16, 3, 3, 3], replicated, may hold values from -0.3125 to 0.3125
- w_third: bfloat16 [64, 32, 3, 3, 3], P('sy'), may hold values from -0.21875 to 0.21875
- feature_grad: bfloat16 [64, 32, 16, 16], P('sy', 'sx'), may hold values from -48 to 48
Outputs:
- features: bfloat16 [64, 32, 16, 16], P('sy', 'sx')
- first_grad: float32 [16, 4, 3, 3, 3], replicated
- second_grad: float32 [32, 16, 3, 3, 3], replicated
- third_grad: float32 [64, 32, 3, 3, 3], P('sy')
All inputs are finite; a program needn't handle non-finite values.
Results may differ from a plain program's by a relative error of at most 0.028.
The roundings to bfloat16 on the way count: a program that leaves them out, or rounds other values in their place, can miss the bound.
Values may be sent and summed in bfloat16 or wider, within the bound.
No kernel may reach another device: no remote copies, remote signals or barrier semaphores. Data moves between devices by JAX's collectives and lax.ppermute only.
A program may use at most 64 MiB of HBM per device.

v0:
```python
import math

import jax
import jax.numpy as jnp
from jax import lax
from jax.sharding import PartitionSpec as P

SLOPE = 0.3


def padded_2(cells, sides, width):
    for axis, dim in sides:
        count = lax.axis_size(axis)
        ends = count - 1
        head = lax.slice_in_dim(cells, 0, width, axis=dim)
        tail = lax.slice_in_dim(cells, cells.shape[dim] - width, cells.shape[dim], axis=dim)
        cells = jnp.concatenate(
            [
                lax.ppermute(tail, axis, [(i, (i + 1) % count) for i in range(ends)]),
                cells,
                lax.ppermute(head, axis, [((i + 1) % count, i) for i in range(ends)]),
            ],
            axis=dim,
        )
    return cells


def leaky_relu(values):
    return jnp.where(values > 0, values, SLOPE * values)


def leaky_slope(values):
    return jnp.where(values > 0, 1.0, SLOPE).astype(jnp.float32)


def pooled_mean(values):
    chans, depths, rows, cols = values.shape
    shaped = values.reshape(chans, depths // 2, 2, rows // 2, 2, cols // 2, 2)
    return jnp.mean(shaped, axis=(2, 4, 6))


def spread(grads):
    finer = jnp.repeat(jnp.repeat(jnp.repeat(grads, 2, axis=1), 2, axis=2), 2, axis=3)
    return finer * 0.125


def width_pad(field):
    return jnp.pad(field, ((0, 0), (0, 0), (0, 0), (1, 1)))


def plane_pad(field):
    return jnp.pad(field, ((0, 0), (0, 0), (1, 1), (1, 1)))


def convolve(padded, kernels):
    depths = padded.shape[1] - 2
    rows = padded.shape[2] - 2
    cols = padded.shape[3] - 2
    stacked = jnp.concatenate([padded[:, :, :, shift : shift + cols] for shift in range(3)], axis=0)
    summed = jnp.zeros((kernels.shape[0], depths, rows, cols), jnp.float32)
    for plane_shift in range(3):
        for row_shift in range(3):
            window = stacked[:, plane_shift : plane_shift + depths, row_shift : row_shift + rows, :]
            matrix = jnp.concatenate(
                [kernels[:, :, plane_shift, row_shift, shift] for shift in range(3)], axis=1
            )
            summed = summed + jnp.einsum(
                "oc,cdhw->odhw", matrix, window, preferred_element_type=jnp.float32
            )
    return summed


def kernel_grad(grads, padded):
    depths = grads.shape[1]
    rows = grads.shape[2]
    cols = grads.shape[3]
    pieces = []
    for plane_shift in range(3):
        for row_shift in range(3):
            for column_shift in range(3):
                window = padded[
                    :,
                    plane_shift : plane_shift + depths,
                    row_shift : row_shift + rows,
                    column_shift : column_shift + cols,
                ]
                pieces.append(
                    jnp.einsum("odhw,cdhw->oc", grads, window, preferred_element_type=jnp.float32)
                )
    stacked = jnp.stack(pieces, axis=-1)
    return stacked.reshape(grads.shape[0], padded.shape[0], 3, 3, 3)


def input_grad(padded_grads, kernels):
    depths = padded_grads.shape[1] - 2
    rows = padded_grads.shape[2] - 2
    cols = padded_grads.shape[3] - 2
    stacked = jnp.concatenate(
        [padded_grads[:, :, :, 2 - shift : 2 - shift + cols] for shift in range(3)], axis=0
    )
    summed = jnp.zeros((kernels.shape[1], depths, rows, cols), jnp.float32)
    for plane_shift in range(3):
        for row_shift in range(3):
            window = stacked[
                :,
                2 - plane_shift : 2 - plane_shift + depths,
                2 - row_shift : 2 - row_shift + rows,
                :,
            ]
            matrix = jnp.concatenate(
                [kernels[:, :, plane_shift, row_shift, shift] for shift in range(3)], axis=0
            )
            summed = summed + jnp.einsum(
                "oc,odhw->cdhw", matrix, window, preferred_element_type=jnp.float32
            )
    return summed


def shards(volume, w_first, w_second, w_third, feature_grad):
    cells = (
        volume.shape[1]
        * volume.shape[2]
        * volume.shape[3]
        * lax.axis_size("sx")
        * lax.axis_size("sy")
    )
    volume_pad = width_pad(padded_2(volume, (("sx", 1), ("sy", 2)), 1))
    first_pre = convolve(volume_pad, w_first)
    first_out = pooled_mean(leaky_relu(first_pre)).astype(jnp.bfloat16)
    first_pad = width_pad(padded_2(first_out, (("sx", 1), ("sy", 2)), 1))
    second_pre = convolve(first_pad, w_second)
    second_out = pooled_mean(leaky_relu(second_pre)).astype(jnp.bfloat16)
    tall_field = lax.all_gather(second_out, "sy", axis=2, tiled=True)
    tall_pad = plane_pad(padded_2(tall_field, (("sx", 1),), 1))
    third_pre = convolve(tall_pad, w_third)
    features = pooled_mean(leaky_relu(third_pre)).astype(jnp.bfloat16)
    third_grads = (leaky_slope(third_pre) * spread(feature_grad.astype(jnp.float32))).astype(
        jnp.bfloat16
    )
    third_wg = kernel_grad(third_grads, tall_pad)
    third_gpad = plane_pad(padded_2(third_grads, (("sx", 1),), 1))
    second_up = lax.psum_scatter(
        input_grad(third_gpad, w_third).astype(jnp.bfloat16), "sy", scatter_dimension=2, tiled=True
    ).astype(jnp.float32)
    second_grads = (leaky_slope(second_pre) * spread(second_up)).astype(jnp.bfloat16)
    second_wg = kernel_grad(second_grads, first_pad)
    second_gpad = width_pad(padded_2(second_grads, (("sx", 1), ("sy", 2)), 1))
    first_up = input_grad(second_gpad, w_second)
    first_grads = (leaky_slope(first_pre) * spread(first_up)).astype(jnp.bfloat16)
    first_wg = kernel_grad(first_grads, volume_pad)
    first_sum, second_sum = lax.psum((first_wg, second_wg), ("sx", "sy"))
    third_sum = lax.psum(third_wg, "sx")
    first_grad = first_sum * (64.0 / math.sqrt(cells))
    second_grad = second_sum * (8.0 / math.sqrt(cells / 8))
    third_grad = third_sum * (1.0 / math.sqrt(cells / 64))
    return (features, first_grad, second_grad, third_grad)


def solution(mesh):
    in_specs = (
        P(None, "sx", "sy", None),
        P(),
        P(),
        P("sy", None, None, None, None),
        P("sy", "sx", None, None),
    )
    out_specs = (P("sy", "sx", None, None), P(), P(), P("sy", None, None, None, None))
    return jax.shard_map(shards, mesh=mesh, in_specs=in_specs, out_specs=out_specs, check_vma=False)
```

profile of v0, /device:TPU:1, one launch (start us, length us, event | category | flops | bytes accessed | tf_op | source)
XLA Modules:
  0.0 588.5 jit_solution(2532351972934428516)
XLA Ops:
  8.1 5.6 collective-permute-start
  20.2 3.8 collective-permute-start.2
  24.0 2.6 collective-permute-start.3
  33.2 2.6 copy.400
  35.8 4.9 reduce_sum.34
  40.9 5.2 collective-permute-start.4
  47.4 5.0 collective-permute-done.5
  52.4 4.1 collective-permute-start.6
  56.5 1.9 collective-permute-start.7
  66.2 21.6 %all_gather.3 = bf16[32,2,32,32]{0,3,2,1:T(8,128)(2,1)S(1)} all-gather(bf16[32,2,2,32]{0,3,2,1:T(8,128)(2,1)S(1)} %multiply_convert_fusion.3), channel_id=1, replica_groups=mesh['sx'=32,'sy'=16] {'sy'}, dimensions={2}, use_global_device_ids=true | all-gather | bytes 139264 | tf_op jit(solution)/shard_map/all_gather | solution.py:133
  87.9 6.5 %collective-permute-start.8 = (bf16[32,1,32,32]{0,3,2,1:T(8,128)(2,1)S(1)}, bf16[32,1,32,32]{0,3,2,1:T(8,128)(2,1)S(1)}, u32[]{:S(2)}, u32[]{:S(2)}) collective-permute-start(bf16[32,1,32,32]{0,3,2,1:T(8,128)(2,1)S(1)} %get-tuple-element.13), channel_id=1, source_target_pairs={{0,16},{16,32},{32,48},{48,64},{64,80},{80,96},{96,112},{112,128},... | collective-permute-start | bytes 196616 | tf_op jit(solution)/shard_map/ppermute | solution.py:19
  94.4 1.5 collective-permute-start.9
  96.0 9.6 %collective-permute-done.8 = bf16[32,1,32,32]{0,3,2,1:T(8,128)(2,1)S(1)} collective-permute-done((bf16[32,1,32,32]{0,3,2,1:T(8,128)(2,1)S(1)}, bf16[32,1,32,32]{0,3,2,1:T(8,128)(2,1)S(1)}, u32[]{:S(2)}, u32[]{:S(2)}) %collective-permute-start.8) | collective-permute-done | bytes 65568 | tf_op jit(solution)/shard_map/ppermute | solution.py:19
  109.0 1.8 convolution_add_fusion.39
  110.8 1.9 convolution_add_fusion.38
  112.7 1.9 convolution_add_fusion.37
  114.6 1.9 convolution_add_fusion.36
  116.4 1.9 convolution_add_fusion.35
  118.3 1.9 convolution_add_fusion.34
  120.2 1.9 convolution_add_fusion.33
  122.0 1.9 convert_reduce_fusion
  135.6 5.6 collective-permute-start.10
  144.1 125.8 %psum.23 = f32[4,32,3,3,3]{1,0,4,3,2:T(4,128)S(1)} all-reduce(f32[4,32,3,3,3]{1,0,4,3,2:T(4,128)S(1)} %bitcast.1188), channel_id=1, replica_groups=mesh['sx'=32,'sy'=16] {'sx'}, use_global_device_ids=true, to_apply=%region_7.8 | all-reduce | flops 3456 | bytes 27648 | tf_op jit(solution)/shard_map/psum | solution.py:152
  275.3 156.7 %all-reduce.9.cloned.1.call-done = bf16[32,2,32,32]{0,3,2,1:T(8,128)(2,1)} async-done(((bf16[32,2,32,32]{0,3,2,1:T(8,128)(2,1)}), bf16[32,2,32,32]{0,3,2,1:T(8,128)(2,1)}) %all-reduce.9.cloned.1.call-update) | async-done | bytes 131088
  437.7 4.3 collective-permute-start.12
  443.5 4.7 collective-permute-done.13
  448.3 1.9 collective-permute-start.14
  450.2 3.4 collective-permute-start.15
  453.9 1.8 collective-permute-done.15
  459.4 2.2 broadcast_in_dim.56
  461.6 2.8 copy.469
  470.8 109.5 %all-reduce.6 = (f32[16,4,3,3,3]{0,1,4,3,2:T(4,128)S(1)}, f32[32,16,3,3,3]{0,1,4,3,2:T(8,128)S(1)}) all-reduce(f32[16,4,3,3,3]{0,1,4,3,2:T(4,128)S(1)} %bitcast.1189, f32[32,16,3,3,3]{0,1,4,3,2:T(8,128)S(1)} %bitcast.1187), channel_id=1, replica_groups=mesh['sx'=32,'sy'=16] {'sx','sy'}, use_global_device_ids=true, to_apply=%region_5.6 | all-reduce | flops 15552 | bytes 124416 | tf_op jit(solution)/shard_map/psum | solution.py:151
  (263 shorter events, 64.3 us)
Async XLA Ops:
  7.2 424.8 %all-reduce.9.cloned.1.call-start = ((), (), s32[]{:S(2)}) async-start(), calls=%async_computation | async-start | bytes 1048576
  8.1 11.2 %collective-permute-start = (bf16[4,1,8,128]{3,0,2,1:T(4,128)(2,1)S(1)}, bf16[4,1,8,128]{3,0,2,1:T(4,128)(2,1)S(1)}, u32[]{:S(2)}, u32[]{:S(2)}) collective-permute-start(bf16[4,1,8,128]{3,0,2,1:T(4,128)(2,1)S(1)} %get-tuple-element.93), channel_id=1, source_target_pairs={{0,16},{16,32},{32,48},{48,64},{64,80},{80,96},{96,112},{112,128},... | collective-permute-start | bytes 24584 | tf_op jit(solution)/shard_map/ppermute | solution.py:19
  13.8 6.4 %collective-permute-start.1 = (bf16[4,1,8,128]{3,0,2,1:T(4,128)(2,1)S(1)}, bf16[4,1,8,128]{3,0,2,1:T(4,128)(2,1)S(1)}, u32[]{:S(2)}, u32[]{:S(2)}) collective-permute-start(bf16[4,1,8,128]{3,0,2,1:T(4,128)(2,1)S(1)} %get-tuple-element.92), channel_id=1, source_target_pairs={{16,0},{32,16},{48,32},{64,48},{80,64},{96,80},{112,96},{128,112},... | collective-permute-start | bytes 24584 | tf_op jit(solution)/shard_map/ppermute | solution.py:21
  20.2 9.7 %collective-permute-start.2 = (bf16[4,10,1,128]{3,0,2,1:T(4,128)(2,1)S(1)}, bf16[4,10,1,128]{3,0,2,1:T(4,128)(2,1)S(1)}, u32[]{:S(2)}, u32[]{:S(2)}) collective-permute-start(bf16[4,10,1,128]{3,0,2,1:T(4,128)(2,1)S(1)} %get-tuple-element.86), channel_id=1, source_target_pairs={{0,1},{1,2},{2,3},{3,4},{4,5},{5,6},{6,7},{7,8},{8,9},{9,10},{10,1... | collective-permute-start | bytes 30728 | tf_op jit(solution)/shard_map/ppermute | solution.py:19
  24.0 5.9 %collective-permute-start.3 = (bf16[4,10,1,128]{3,0,2,1:T(4,128)(2,1)S(1)}, bf16[4,10,1,128]{3,0,2,1:T(4,128)(2,1)S(1)}, u32[]{:S(2)}, u32[]{:S(2)}) collective-permute-start(bf16[4,10,1,128]{3,0,2,1:T(4,128)(2,1)S(1)} %get-tuple-element.87), channel_id=1, source_target_pairs={{1,0},{2,1},{3,2},{4,3},{5,4},{6,5},{7,6},{8,7},{9,8},{10,9},{11,1... | collective-permute-start | bytes 30728 | tf_op jit(solution)/shard_map/ppermute | solution.py:21
  35.8 11.6 %copy-start.2 = (bf16[4,32,3,3,3]{1,0,4,3,2:T(4,128)(2,1)S(1)}, bf16[4,32,3,3,3]{1,0,4,3,2:T(4,128)(2,1)}, u32[]{:S(2)}) copy-start(bf16[4,32,3,3,3]{1,0,4,3,2:T(4,128)(2,1)} %param.8) | copy-start | bytes 20740
  40.9 6.5 %collective-permute-start.4 = (bf16[16,1,4,64]{3,0,2,1:T(8,128)(2,1)S(1)}, bf16[16,1,4,64]{3,0,2,1:T(8,128)(2,1)S(1)}, u32[]{:S(2)}, u32[]{:S(2)}) collective-permute-start(bf16[16,1,4,64]{3,0,2,1:T(8,128)(2,1)S(1)} %get-tuple-element.90), channel_id=1, source_target_pairs={{0,16},{16,32},{32,48},{48,64},{64,80},{80,96},{96,112},{112,128},... | collective-permute-start | bytes 24584 | tf_op jit(solution)/shard_map/ppermute | solution.py:19
  46.1 6.3 %collective-permute-start.5 = (bf16[16,1,4,64]{3,0,2,1:T(8,128)(2,1)S(1)}, bf16[16,1,4,64]{3,0,2,1:T(8,128)(2,1)S(1)}, u32[]{:S(2)}, u32[]{:S(2)}) collective-permute-start(bf16[16,1,4,64]{3,0,2,1:T(8,128)(2,1)S(1)} %get-tuple-element.91), channel_id=1, source_target_pairs={{16,0},{32,16},{48,32},{64,48},{80,64},{96,80},{112,96},{128,112},... | collective-permute-start | bytes 24584 | tf_op jit(solution)/shard_map/ppermute | solution.py:21
  52.4 10.7 %collective-permute-start.6 = (bf16[16,6,1,64]{3,0,2,1:T(8,128)(2,1)S(1)}, bf16[16,6,1,64]{3,0,2,1:T(8,128)(2,1)S(1)}, u32[]{:S(2)}, u32[]{:S(2)}) collective-permute-start(bf16[16,6,1,64]{3,0,2,1:T(8,128)(2,1)S(1)} %get-tuple-element.84), channel_id=1, source_target_pairs={{0,1},{1,2},{2,3},{3,4},{4,5},{5,6},{6,7},{7,8},{8,9},{9,10},{10,1... | collective-permute-start | bytes 36872 | tf_op jit(solution)/shard_map/ppermute | solution.py:19
  56.5 6.6 %collective-permute-start.7 = (bf16[16,6,1,64]{3,0,2,1:T(8,128)(2,1)S(1)}, bf16[16,6,1,64]{3,0,2,1:T(8,128)(2,1)S(1)}, u32[]{:S(2)}, u32[]{:S(2)}) collective-permute-start(bf16[16,6,1,64]{3,0,2,1:T(8,128)(2,1)S(1)} %get-tuple-element.85), channel_id=1, source_target_pairs={{1,0},{2,1},{3,2},{4,3},{5,4},{6,5},{7,6},{8,7},{9,8},{10,9},{11,1... | collective-permute-start | bytes 36872 | tf_op jit(solution)/shard_map/ppermute | solution.py:21
  87.9 17.7 %collective-permute-start.8 = (bf16[32,1,32,32]{0,3,2,1:T(8,128)(2,1)S(1)}, bf16[32,1,32,32]{0,3,2,1:T(8,128)(2,1)S(1)}, u32[]{:S(2)}, u32[]{:S(2)}) collective-permute-start(bf16[32,1,32,32]{0,3,2,1:T(8,128)(2,1)S(1)} %get-tuple-element.13), channel_id=1, source_target_pairs={{0,16},{16,32},{32,48},{48,64},{64,80},{80,96},{96,112},{112,128},... | collective-permute-start | bytes 196616 | tf_op jit(solution)/shard_map/ppermute | solution.py:19
  94.4 11.1 %collective-permute-start.9 = (bf16[32,1,32,32]{0,3,2,1:T(8,128)(2,1)S(1)}, bf16[32,1,32,32]{0,3,2,1:T(8,128)(2,1)S(1)}, u32[]{:S(2)}, u32[]{:S(2)}) collective-permute-start(bf16[32,1,32,32]{0,3,2,1:T(8,128)(2,1)S(1)} %get-tuple-element.14), channel_id=1, source_target_pairs={{16,0},{32,16},{48,32},{64,48},{80,64},{96,80},{112,96},{128,112},... | collective-permute-start | bytes 196616 | tf_op jit(solution)/shard_map/ppermute | solution.py:21
  108.0 1.0 copy-start
  135.6 134.2 %collective-permute-start.10 = (bf16[4,1,32,32]{3,0,2,1:T(4,128)(2,1)S(1)}, bf16[4,1,32,32]{3,0,2,1:T(4,128)(2,1)S(1)}, u32[]{:S(2)}, u32[]{:S(2)}) collective-permute-start(bf16[4,1,32,32]{3,0,2,1:T(4,128)(2,1)S(1)} %get-tuple-element.88), channel_id=1, source_target_pairs={{0,16},{16,32},{32,48},{48,64},{64,80},{80,96},{96,112},{112,128},... | collective-permute-start | bytes 24584 | tf_op jit(solution)/shard_map/ppermute | solution.py:19
  141.2 128.6 %collective-permute-start.11 = (bf16[4,1,32,32]{3,0,2,1:T(4,128)(2,1)S(1)}, bf16[4,1,32,32]{3,0,2,1:T(4,128)(2,1)S(1)}, u32[]{:S(2)}, u32[]{:S(2)}) collective-permute-start(bf16[4,1,32,32]{3,0,2,1:T(4,128)(2,1)S(1)} %get-tuple-element.89), channel_id=1, source_target_pairs={{16,0},{32,16},{48,32},{64,48},{80,64},{96,80},{112,96},{128,112},... | collective-permute-start | bytes 24584 | tf_op jit(solution)/shard_map/ppermute | solution.py:21
  437.7 5.8 collective-permute-start.12
  442.1 6.2 %collective-permute-start.13 = (bf16[32,1,4,64]{3,0,2,1:T(8,128)(2,1)S(1)}, bf16[32,1,4,64]{3,0,2,1:T(8,128)(2,1)S(1)}, u32[]{:S(2)}, u32[]{:S(2)}) collective-permute-start(bf16[32,1,4,64]{3,0,2,1:T(8,128)(2,1)S(1)} %get-tuple-element.27), channel_id=1, source_target_pairs={{16,0},{32,16},{48,32},{64,48},{80,64},{96,80},{112,96},{128,112},... | collective-permute-start | bytes 49160 | tf_op jit(solution)/shard_map/ppermute | solution.py:21
  448.3 5.6 collective-permute-start.14
  450.2 5.4 collective-permute-start.15
  466.1 1.4 copy-start.1
Sparse Core Ops, SparseCore 0:
  274.7 157.1 all-reduce.8
where the time goes:
time: 590 us; the launch traced here: 588 us
  blocking collectives  257 us (44%)
  waiting for transfers between devices  178 us (30%)
  starting transfers between devices  51.7 us (9%)
  matrix products  48 us (8%)
  local copies, waits for them, and re-layouts  25.9 us (4%)
  between operations  15.5 us (3%)
  other arithmetic  12.7 us (2%)
    unnamed x2, waiting for transfers between devices  157 us
    psum x1, blocking collectives, shards(): third_sum = lax.psum(third_wg, 'sx')  126 us
    psum x1, blocking collectives, shards(): first_sum, second_sum = lax.psum((first_wg, second_wg), ('sx', 'sy'))  110 us
    ppermute x8, starting transfers between devices, padded_2(): lax.ppermute(tail, axis, [(i, (i + 1) % count) for i in range(ends)])  37.1 us
    dot_general x81, matrix products, kernel_grad(): jnp.einsum('odhw,cdhw->oc', grads, window, preferred_element_type=jnp.flo...  22.6 us
    all_gather x1, blocking collectives, shards(): tall_field = lax.all_gather(second_out, 'sy', axis=2, tiled=True)  21.6 us
    dot_general x27, matrix products, convolve(): jnp.einsum('oc,cdhw->odhw', matrix, window, preferred_element_type=jnp.fl...  20.3 us
    ppermute x8, starting transfers between devices, padded_2(): lax.ppermute(head, axis, [((i + 1) % count, i) for i in range(ends)])  14.6 us
  transfers between devices with their start and end apart: 17, of which 5 were waited for; matrix products, arithmetic and copies ran while one was open for 3% of the time, Pallas kernels for 0%

commit v1 on v0

v1 whole, which is shorter than its diff:
```python
import math

import jax
import jax.numpy as jnp
import numpy as np
from jax import lax
from jax.experimental import pallas as pl
from jax.experimental.pallas import tpu as pltpu
from jax.sharding import PartitionSpec as P

SLOPE = 0.3
BF16 = jnp.bfloat16
F32 = jnp.float32


def tap_shift(rows, cols, out_first, out_rows):
    table = np.zeros((rows, cols, 3, 3, out_rows, cols), np.float32)
    for kh in range(3):
        for kw in range(3):
            for r in range(out_rows):
                for w in range(cols):
                    row, col = out_first + r + kh - 1, w + kw - 1
                    if 0 <= row < rows and 0 <= col < cols:
                        table[row, col, kh, kw, r, w] = 1
    return table.reshape(rows * cols, 9 * out_rows * cols)


def second_spread():
    table = np.zeros((8, 32, 8, 64), np.float32)
    for r in range(8):
        for w in range(64):
            table[2 + r // 2, w // 2, r, w] = 0.125
    return table.reshape(256, 512)


def block_taps():
    table = np.zeros((2, 2, 2, 4, 4, 4, 4, 128), np.float32)
    for pd, ph, pw in np.ndindex(2, 2, 2):
        for kd, kh, kw, c in np.ndindex(3, 3, 3, 4):
            at = ((kd * 3 + kh) * 3 + kw) * 4 + c
            table[pd, ph, pw, kd + pd, kw + pw, kh + ph, c, at] = 1
    return table.reshape(2048, 128)


def dot(a, b):
    return lax.dot_general(a, b, (((1,), (0,)), ((), ())), preferred_element_type=F32)


def dot_t(a, b):
    return lax.dot_general(a, b, (((1,), (1,)), ((), ())), preferred_element_type=F32)


def placed(shape, match, value=1.0, dtype=BF16):
    row, lane = (lax.broadcasted_iota(jnp.int32, shape, axis) for axis in range(2))
    return jnp.where(match(row, lane), value, 0.0).astype(dtype)


def unit(size, dtype):
    return placed((size, size), lambda row, lane: row == lane, 1.0, dtype)


def turned():
    return placed((32, 32), lambda row, lane: lane == (row & 3) * 8 + (row >> 2))


def column_shift(cols):
    def match(row, lane):
        to = (lane & 127) + (lane >> 7) - 1
        return jnp.logical_and(row == to, (row // cols) == (lane & 127) // cols)

    return placed((128, 384), match)


def column_pairs():
    return placed((128, 512), lambda row, lane: row == 2 * (lane & 63) + (lane >> 7) - 1)


def second_pool():
    return placed((512, 128), lambda row, lane: lane == (row >> 7) * 32 + ((row & 63) >> 1), 0.125)


def third_pool():
    def match(row, lane):
        inside = jnp.logical_and(row >= 96, row < 160)
        return jnp.logical_and(inside, lane == ((row & 31) >> 1))

    return placed((256, 128), match, 0.125)


def feature_spread():
    def match(row, lane):
        inside = jnp.logical_and(lane >= 32, lane < 224)
        return jnp.logical_and(inside, row == ((lane - 32) >> 6) * 16 + ((lane & 31) >> 1))

    return placed((128, 256), match, 0.125)


def brick_join():
    def match(row, lane):
        return row == lane + jnp.where(lane < 64, 0, jnp.where(lane < 192, 64, 128))

    return placed((384, 256), match)


def dot_two(a, b):
    high = a.astype(BF16)
    low = (a - high.astype(F32)).astype(BF16)
    out = dot(jnp.concatenate([high, low], axis=0), b)
    return out[: a.shape[0]] + out[a.shape[0] :]


def leaky(values):
    return jnp.where(values > 0, values, SLOPE * values)


def lanes(count):
    return lax.broadcasted_iota(jnp.int32, (1, count), 1)


def turned_field(volume_in, grads_in, field, volume, feature_grad, held, done):
    pairs = ((volume_in, volume), (grads_in, feature_grad))
    copies = [pltpu.make_async_copy(a, b, done.at[i]) for i, (a, b) in enumerate(pairs)]
    for copy in copies:
        copy.start()
    held[...] = jnp.zeros(held.shape, F32)
    turn = turned()
    copies[1].wait()
    grads = feature_grad[...].astype(F32)
    for s in range(16):
        for i in range(3):
            h = s + i - 1
            if 0 <= h < 16:
                held[4 * s : 4 * s + 4, 16 * i : 16 * i + 16] = grads[:, h, :]
    for t in range(2):
        field[8 + t] = held[32 * t : 32 * t + 32].astype(BF16)
    copies[0].wait()
    for d in range(8):
        stack = jnp.concatenate([volume[c, d].astype(F32) for c in range(4)], axis=0)
        field[d] = dot(turn, stack.astype(BF16)).astype(BF16)


def tall_field(w_third, far_prev, prev, own, nxt, far_nxt, tall, sent, held):
    for d in range(7):
        tall[d] = far_prev[d + 1]
        tall[31 + d] = far_nxt[d]
    for d in range(8):
        tall[7 + d] = prev[d]
        tall[15 + d] = own[d]
        tall[23 + d] = nxt[d]
    held[...] = jnp.zeros(held.shape, F32)
    for k in range(27):
        g, i = divmod(k, 4)
        held[0, 4 * g : 4 * g + 4, 32 * i : 32 * i + 32] = w_third[k].astype(F32)
    for s in range(1, 16):
        held[s, 0:28] = held[0, 0:28]
    for j, part in enumerate((prev, own, nxt)):
        for t in range(2):
            grads = part[8 + t].astype(F32)
            for s in range(8):
                held[8 * t + s, 28 + 4 * j : 32 + 4 * j] = grads[4 * s : 4 * s + 4]
    sent[...] = held[...].astype(BF16)


def forward(
    n_sx, field, w_first, w_second, taps,
    second, mask_a, patch_a, mask_b, patch_b, cells, rows_b, cols,
):
    ix, iy = lax.axis_index("sx"), lax.axis_index("sy")
    left = lanes(128) < 64
    flat = field[...].reshape(3648, 128)
    pairs = column_pairs()
    for half in range(2):
        wide = dot(flat, pairs[:, 256 * half : 256 * half + 256])
        for t in range(2):
            for d in range(38):
                part = wide[96 * d : 96 * d + 96, 128 * t : 128 * t + 128]
                cells[2 * half + t, d] = jnp.where(left, part[0:80], part[8:88]).astype(BF16)
    turned_w = dot_t(unit(16, BF16), w_first[...]).astype(BF16)
    w_a = jnp.concatenate(
        [dot_t(turned_w, taps[256 * p : 256 * p + 256]).astype(BF16) for p in range(8)], axis=0
    )
    w_b = dot_t(unit(32, BF16), w_second[...]).astype(BF16)
    pair = lanes(128) // 64
    for two in range(9):
        rows = []
        for kd in range(4):
            for t in range(4):
                pieces = []
                for d in (2 * two, 2 * two + 1):
                    for a in range(5):
                        pieces.append(cells[t, 2 * d + kd, 16 * a : 16 * a + 16])
                rows.append(jnp.concatenate(pieces, axis=1))
        patch = jnp.concatenate(rows, axis=0)
        pre = dot(w_a, patch)
        act = leaky(pre)
        pool = act[0:16]
        for p in range(1, 8):
            pool = pool + act[16 * p : 16 * p + 16]
        pool = 0.125 * pool
        for t in range(2):
            d = 2 * two + t
            start = 640 * t
            if 7 <= d < 11:
                own = pre[:, start + 128 : start + 512]
                mask_a[d - 7] = jnp.where(own > 0, 1.0, 0.0).astype(BF16)
                patch_a[d - 7] = patch[:, start + 128 : start + 512]
            deep = 4 * ix - 7 + d
            in_depth = jnp.logical_and(deep >= 0, deep < 4 * n_sx)
            kept = []
            for a in range(5):
                row = 4 * iy - 3 + 2 * a + pair
                keep = jnp.logical_and(jnp.logical_and(row >= 0, row < 64), in_depth)
                kept.append(jnp.where(keep, pool[:, start + 128 * a : start + 128 * a + 128], 0.0))
            kept = jnp.concatenate(kept, axis=0)
            swapped = pltpu.roll(kept, 64, 1)
            odd = jnp.where(left, swapped[0:64], swapped[16:80])
            rows_b[d] = jnp.concatenate([kept, odd], axis=0).astype(BF16)
    wide = dot(rows_b[...].reshape(2592, 128), column_shift(64)).astype(BF16)
    for d in range(18):
        for kh in range(3):
            first = 144 * d + 16 * (0, 5, 1)[kh]
            for kw in range(3):
                block = jnp.concatenate(
                    [
                        wide[first + 16 * j : first + 16 * j + 16, 128 * kw : 128 * kw + 128]
                        for j in range(4)
                    ],
                    axis=1,
                )
                cols[d, 16 * (3 * kh + kw) : 16 * (3 * kh + kw) + 16] = block
    for d in range(6):
        patch_b[d] = cols[d + 6]
    row = 2 * iy - 1 + lanes(128) // 32
    in_rows = jnp.logical_and(row >= 0, row < 32)
    acts = []
    for e in range(8):
        act = jnp.zeros((32, 512), F32)
        for d in (2 * e, 2 * e + 1):
            pre = dot(w_b, cols[d : d + 3].reshape(432, 512))
            if 4 <= d < 12:
                mask_b[d - 4] = jnp.where(pre > 0, 1.0, 0.0).astype(BF16)
            act = act + leaky(pre)
        acts.append(act)
    pool = dot_two(jnp.concatenate(acts, axis=0), second_pool())
    for e in range(8):
        deep = 2 * ix - 3 + e
        in_depth = jnp.logical_and(deep >= 0, deep < 2 * n_sx)
        out = pool[32 * e : 32 * e + 32]
        second[e] = jnp.where(jnp.logical_and(in_rows, in_depth), out, 0.0).astype(BF16)


def backward(
    n_sx, prev, own, nxt, got, mask_a, patch_a, mask_b, patch_b, w_second, taps,
    shift_c, shift_d, spread_b,
    parts, w_third, grads, cols_c, grads_c, cols_g, flip_c, flip_b, grads_b, cols_h, held,
):
    ix, iy = lax.axis_index("sx"), lax.axis_index("sy")
    arrived = got[...].astype(F32)
    for s in range(16):
        for g in range(7):
            w_third[4 * s : 4 * s + 4, 128 * g : 128 * g + 128] = arrived[s, 4 * g : 4 * g + 4]
        for j in range(3):
            grads[j, 4 * s : 4 * s + 4] = arrived[s, 28 + 4 * j : 32 + 4 * j]
    wide_w = w_third[...].astype(BF16)
    w_c = wide_w[:, 0:864]
    tall = jnp.concatenate([prev[...], own[...], nxt[...]], axis=2).reshape(256, 384)
    joined = dot(tall, brick_join()).astype(BF16)
    for k in range(9):
        shifted = dot(joined, shift_c[:, 256 * k : 256 * k + 256]).astype(BF16)
        for d in range(8):
            cols_c[d, 32 * k : 32 * k + 32] = shifted[32 * d : 32 * d + 32]
    row = lanes(256) // 32
    mine = jnp.logical_and(row >= 3, row < 5)
    spread_c = feature_spread()
    spreads = [dot(grads[j].astype(BF16), spread_c) for j in range(3)]
    pooled = jnp.zeros((64, 256), F32)
    third_wg = jnp.zeros((64, 864), F32)
    for e in range(1, 7):
        window = cols_c[e - 1 : e + 2].reshape(864, 256)
        pre = dot(w_c, window)
        back = (jnp.where(pre > 0, 1.0, SLOPE) * spreads[(e - 1) // 2]).astype(BF16)
        grads_c[e - 1] = back
        if e in (3, 4):
            pooled = pooled + leaky(pre)
            third_wg = third_wg + dot_t(jnp.where(mine, back, jnp.zeros((), BF16)), window)
    features = dot_two(pooled, third_pool())
    for k in range(9):
        shifted = dot(grads_c[...].reshape(384, 256), shift_c[:, 256 * k : 256 * k + 256])
        shifted = shifted.astype(BF16)
        for e in range(6):
            cols_g[e, 64 * k : 64 * k + 64] = shifted[64 * e : 64 * e + 64]
    for j in range(27):
        k = 26 - j
        flip_c[64 * j : 64 * j + 64, :] = w_third[:, 32 * k : 32 * k + 32]
    back_c = dot_t(unit(32, BF16), flip_c[...].astype(BF16)).astype(BF16)
    ups = [dot(back_c, cols_g[e : e + 3].reshape(1728, 256)) for e in range(4)]
    fine = dot_two(jnp.concatenate(ups, axis=0), spread_b[...])
    row = 4 * iy - 2 + lanes(512) // 64
    in_rows = jnp.logical_and(row >= 0, row < 64)
    row = lanes(512) // 64
    mine = jnp.logical_and(row >= 2, row < 6)
    second_wg = jnp.zeros((32, 432), F32)
    for d in range(1, 7):
        slope = jnp.where(mask_b[d].astype(F32) > 0.5, 1.0, SLOPE)
        deep = 4 * ix - 2 + d
        keep = jnp.logical_and(in_rows, jnp.logical_and(deep >= 0, deep < 4 * n_sx))
        back = jnp.where(keep, slope * fine[32 * (d // 2) : 32 * (d // 2) + 32], 0.0)
        if 2 <= d < 6:
            own_part = jnp.where(mine, back, 0.0).astype(BF16)
            second_wg = second_wg + dot_t(own_part, patch_b[d - 2 : d + 1].reshape(432, 512))
        grads_b[d - 1] = back.astype(BF16)
    for k in range(9):
        shifted = dot(grads_b[...].reshape(192, 512), shift_d[:, 256 * k : 256 * k + 256])
        shifted = shifted.astype(BF16)
        for d in range(6):
            cols_h[d, 32 * k : 32 * k + 32] = shifted[32 * d : 32 * d + 32]
    wb = w_second[...].astype(F32)
    for j in range(27):
        k = 26 - j
        flip_b[:, 32 * j : 32 * j + 32] = wb[16 * k : 16 * k + 16]
    back_b = flip_b[...][:, 0:864].astype(BF16)
    ups = [dot(back_b, cols_h[d : d + 3].reshape(864, 256)) for d in range(4)]
    left = lanes(128) < 64
    blocks = jnp.zeros((128, 256), F32)
    for d in range(4):
        one, two = (pltpu.roll(0.125 * ups[d][:, 128 * t : 128 * t + 128], 64, 1) for t in range(2))
        up = jnp.concatenate(
            [jnp.where(left, 0.0, one), jnp.where(left, one, two), jnp.where(left, two, 0.0)], axis=1
        )
        slope = jnp.where(mask_a[d].astype(F32) > 0.5, 1.0, SLOPE)
        back = (slope * jnp.concatenate([up] * 8, axis=0)).astype(BF16)
        blocks = blocks + dot_t(back, patch_a[d])
    first_wg = jnp.zeros((16, 128), F32)
    for p in range(8):
        first_wg = first_wg + dot_two(
            blocks[16 * p : 16 * p + 16], taps[256 * p : 256 * p + 256]
        )
    third_wg = jnp.concatenate([third_wg, jnp.zeros((64, 32), F32)], axis=1)
    second_wg = jnp.concatenate([second_wg, jnp.zeros((32, 80), F32)], axis=1)
    held[...] = jnp.zeros(held.shape, F32)
    for q in range(32):
        hi, s = divmod(q, 16)
        for g in range(7):
            o = 4 * s + 2 * hi
            held[q, 2 * g : 2 * g + 2] = third_wg[o : o + 2, 128 * g : 128 * g + 128]
        for g in range(4):
            held[q, 14 + g : 15 + g] = second_wg[q : q + 1, 128 * g : 128 * g + 128]
        if hi == 0:
            held[q, 18:19] = first_wg[s : s + 1]
        held[q, 19:23] = features[4 * s : 4 * s + 4]
    parts[...] = held[...].astype(BF16)


def summed(got):
    total = got[0].astype(F32)
    for s in range(1, got.shape[0]):
        total = total + got[s].astype(F32)
    return total


def spread_sum(got, total):
    out = summed(got).astype(BF16)
    for s in range(total.shape[0]):
        total[s] = out


def plane_sum(got, total, features, held):
    spread_sum(got, total)
    hi = lax.rem(lax.axis_index("sx"), 2)
    arrived = got[pl.ds(16 * hi, 16)].astype(F32)
    for o in range(4):
        for s in range(16):
            held[o, s : s + 1] = arrived[s, 19 + o : 20 + o, 0:16]
    features[...] = held[...].astype(BF16)


def last(scale_a, scale_b, scale_c, got, first, second, third, held_a, held_b):
    held_a[...] = jnp.zeros(held_a.shape, F32)
    held_b[...] = jnp.zeros(held_b.shape, F32)
    for q in range(32):
        part = got[q].astype(F32)
        if q < 16:
            held_a[q : q + 1] = part[18:19]
        for g in range(4):
            held_b[q : q + 1, 128 * g : 128 * g + 128] = part[14 + g : 15 + g]
    for hi in range(2):
        part = scale_c * got[16 * hi + lax.axis_index("sy")].astype(F32)
        for k in range(27):
            g, i = divmod(k, 4)
            third[k, 2 * hi : 2 * hi + 2] = part[2 * g : 2 * g + 2, 32 * i : 32 * i + 32]
    turned_a = scale_a * jnp.transpose(held_a[...])
    for k in range(27):
        first[k] = turned_a[4 * k : 4 * k + 4, 0:16]
    for g in range(4):
        turned_b = scale_b * jnp.transpose(held_b[:, 128 * g : 128 * g + 128])
        for j in range(8):
            k = 8 * g + j
            if k < 27:
                second[k] = turned_b[16 * j : 16 * j + 16, 0:32]


def call(body, outs, scratch, *args, space=pltpu.VMEM, copies=0, limit=48 * 1024 * 1024, cost=1e8):
    semaphores = [pltpu.SemaphoreType.DMA((copies,))] if copies else []
    return pl.pallas_call(
        body,
        out_shape=[jax.ShapeDtypeStruct(shape, dtype) for shape, dtype in outs],
        in_specs=[pl.BlockSpec(memory_space=space)] * len(args),
        out_specs=[pl.BlockSpec(memory_space=pltpu.VMEM)] * len(outs),
        scratch_shapes=[pltpu.VMEM(shape, dtype) for shape, dtype in scratch] + semaphores,
        compiler_params=pltpu.CompilerParams(vmem_limit_bytes=limit),
        cost_estimate=pl.CostEstimate(flops=int(cost), bytes_accessed=10**5, transcendentals=0),
    )(*args)


def exchanged(to_prev, to_next, axis, step=1):
    ends = lax.axis_size(axis) - step
    from_prev = lax.ppermute(to_next, axis, [(i, i + step) for i in range(ends)])
    from_next = lax.ppermute(to_prev, axis, [(i + step, i) for i in range(ends)])
    return from_prev, from_next


def table(values, dtype=BF16):
    return jnp.asarray(values, dtype)


def shards(volume, w_first, w_second, w_third, feature_grad):
    n_sx, n_sy = lax.axis_size("sx"), lax.axis_size("sy")
    n_z = n_sx // 2
    cells = volume.shape[1] * volume.shape[2] * volume.shape[3] * n_sx * n_sy
    first_w = jnp.pad(w_first.transpose(2, 3, 4, 1, 0).reshape(108, 16), ((0, 20), (0, 0)))
    second_w = w_second.transpose(2, 3, 4, 1, 0).reshape(432, 32)
    third_w = w_third.transpose(2, 3, 4, 0, 1).reshape(27, 4, 32)
    taps = table(block_taps())

    (field,) = call(
        turned_field,
        [((10, 32, 128), BF16)],
        [((4, 8, 8, 128), BF16), ((4, 16, 16), BF16), ((64, 128), F32)],
        volume, feature_grad.reshape(4, 16, 16),
        space=pl.ANY, copies=2, limit=None,
    )
    prev, nxt = exchanged(field, field, "sx")
    far_prev, far_nxt = exchanged(field[:8], field[:8], "sx", 2)
    tall, sent = call(
        tall_field,
        [((38, 32, 128), BF16), ((16, 40, 128), BF16)],
        [((16, 40, 128), F32)],
        third_w, far_prev, prev, field, nxt, far_nxt,
    )
    got = lax.all_to_all(sent, "sy", 0, 0, tiled=True)
    prev, nxt = exchanged(tall, tall, "sy")
    field = jnp.concatenate([prev[:, 4:], tall, nxt, nxt[:, :4]], axis=1)
    second, mask_a, patch_a, mask_b, patch_b = call(
        lambda *refs: forward(n_sx, *refs),
        [
            ((8, 32, 128), BF16), ((4, 128, 384), BF16), ((4, 256, 384), BF16),
            ((8, 32, 512), BF16), ((6, 144, 512), BF16),
        ],
        [((4, 38, 80, 128), BF16), ((18, 144, 128), BF16), ((18, 144, 512), BF16)],
        field, first_w, second_w, taps, cost=5e9,
    )
    prev, nxt = exchanged(second, second, "sy")
    (parts,) = call(
        lambda *refs: backward(n_sx, *refs),
        [((32, 24, 128), BF16)],
        [
            ((64, 896), F32), ((3, 64, 128), F32), ((8, 288, 256), BF16), ((6, 64, 256), BF16),
            ((6, 576, 256), BF16), ((1728, 32), F32), ((16, 896), F32),
            ((6, 32, 512), BF16), ((6, 288, 256), BF16), ((32, 24, 128), F32),
        ],
        prev, second, nxt, got, mask_a, patch_a, mask_b, patch_b, second_w, taps,
        table(tap_shift(8, 32, 0, 8)), table(tap_shift(8, 64, 2, 4)),
        table(second_spread()), cost=11e9,
    )
    planes = [[32 * z + i for i in range(32)] for z in range(n_z)]
    lines = [[2 * z + hi for z in range(n_z)] for hi in range(2)]
    both = ("sx", "sy")
    got = lax.all_to_all(parts, both, 0, 0, tiled=True, axis_index_groups=planes)
    total, features = call(
        plane_sum, [((n_z, 24, 128), BF16), ((4, 16, 16), BF16)], [((4, 16, 16), F32)], got
    )
    got = lax.all_to_all(total, "sx", 0, 0, tiled=True, axis_index_groups=lines)
    (total,) = call(spread_sum, [((32, 24, 128), BF16)], [], got)
    got = lax.all_to_all(total, both, 0, 0, tiled=True, axis_index_groups=planes)
    scales = (64.0 / math.sqrt(cells), 8.0 / math.sqrt(cells / 8), 1.0 / math.sqrt(cells / 64))
    first, second, third = call(
        lambda *refs: last(*scales, *refs),
        [((27, 4, 16), F32), ((27, 16, 32), F32), ((27, 4, 32), F32)],
        [((128, 128), F32), ((128, 512), F32)],
        got,
    )
    first_grad = first.reshape(3, 3, 3, 4, 16).transpose(4, 3, 0, 1, 2)
    second_grad = second.reshape(3, 3, 3, 16, 32).transpose(4, 3, 0, 1, 2)
    third_grad = third.reshape(3, 3, 3, 4, 32).transpose(3, 4, 0, 1, 2)
    return (features.reshape(4, 1, 16, 16), first_grad, second_grad, third_grad)


def solution(mesh):
    in_specs = (
        P(None, "sx", "sy", None),
        P(),
        P(),
        P("sy", None, None, None, None),
        P("sy", "sx", None, None),
    )
    out_specs = (P("sy", "sx", None, None), P(), P(), P("sy", None, None, None, None))
    return jax.shard_map(shards, mesh=mesh, in_specs=in_specs, out_specs=out_specs, check_vma=False)
```

time: 590 us -> 122 us (0.21)
  blocking collectives: 257 us -> 59.4 us
  waiting for transfers between devices: 178 us -> 2.61 us
  matrix products: 48 us -> 0 us
  starting transfers between devices: 51.7 us -> 34 us
  local copies, waits for them, and re-layouts: 25.9 us -> 8.82 us
  Pallas kernels: 0 us -> 15 us
  between operations: 15.5 us -> 0.84 us
  other arithmetic: 12.7 us -> 0.35 us
    psum x2 -> x0, blocking collectives: 235 us -> none  [the longest x1 126 us: shards(): third_sum = lax.psum(third_wg, 'sx')]
    unnamed x2 -> x0, waiting for transfers between devices: 157 us -> none
    all_to_all x0 -> x3, blocking collectives: none -> 59.4 us  [the longest x1 29.4 us: shards(): got = lax.all_to_all(total, 'sx', 0, 0, tiled=True, axis_index_groups=lines)]
    dot_general x126 -> x0, matrix products: 48 us -> none  [the longest x81 22.6 us: kernel_grad(): jnp.einsum('odhw,cdhw->oc', grads, window, preferred_element_type=jnp.flo...]
    all_gather x1 -> x0, blocking collectives: 21.6 us -> none  [shards(): tall_field = lax.all_gather(second_out, 'sy', axis=2, tiled=True)]
    ppermute x16 -> x8, starting transfers between devices: 51.6 us -> 30.1 us  [the longest x4 15.9 us: exchanged(): lax.ppermute(to_next, axis, [(i, i + step) for i in range(ends)])]
    ppermute x16 -> x8, waiting for transfers between devices: 21.1 us -> 2.61 us  [the longest x4 2.59 us: exchanged(): lax.ppermute(to_next, axis, [(i, i + step) for i in range(ends)])]
    pallas_call x0 -> x7, Pallas kernels: none -> 15 us  [call(): pl.pallas_call(body, out_shape=[jax.ShapeDtypeStruct(shape, dtype) for sh...]
  transfers between devices with their start and end apart: 17 -> 9, of which waited for: 5 -> 2; matrix products, arithmetic and copies ran while one was open for 3% -> 2% of each run, Pallas kernels for 0% -> 4%
where the time goes in v1:
time: 122 us; the launch traced here: 121 us
  blocking collectives  59.4 us (49%)
  starting transfers between devices  34 us (28%)
  Pallas kernels  15 us (12%)
  local copies, waits for them, and re-layouts  8.82 us (7%)
  waiting for transfers between devices  2.61 us (2%)
    all_to_all x1, blocking collectives, shards(): got = lax.all_to_all(total, 'sx', 0, 0, tiled=True, axis_index_groups=lines)  29.4 us
    all_to_all x1, blocking collectives, shards(): lax.all_to_all(parts, both, 0, 0, tiled=True, axis_index_groups=planes)  16.1 us
    ppermute x4, starting transfers between devices, exchanged(): lax.ppermute(to_next, axis, [(i, i + step) for i in range(ends)])  15.9 us
    pallas_call x7, Pallas kernels, call(): pl.pallas_call(body, out_shape=[jax.ShapeDtypeStruct(shape, dtype) for sh...  15 us
    ppermute x4, starting transfers between devices, exchanged(): lax.ppermute(to_prev, axis, [(i + step, i) for i in range(ends)])  14.3 us
    all_to_all x1, blocking collectives, shards(): lax.all_to_all(total, both, 0, 0, tiled=True, axis_index_groups=planes)  13.9 us
    unnamed x24, local copies, waits for them, and re-layouts  7.06 us
    all_to_all x1, starting transfers between devices, shards(): got = lax.all_to_all(sent, 'sy', 0, 0, tiled=True)  3.83 us
  transfers between devices with their start and end apart: 9, of which 2 were waited for; matrix products, arithmetic and copies ran while one was open for 2% of the time, Pallas kernels for 4%

profile of v1, /device:TPU:1, one launch (start us, length us, event | category | flops | bytes accessed | tf_op | source)
XLA Modules:
  0.0 121.0 jit_solution(2816025718004496054)
XLA Ops:
  0.6 1.7 %shard_map.120.own = bf16[10,32,128]{2,1,0:T(8,128)(2,1)} custom-call(bf16[4,8,8,128]{3,2,1,0:T(8,128)(2,1)} %volume_in.1, bf16[4,16,16]{2,1,0:T(8,128)(2,1)} %bitcast.24), custom_call_target="tpu_custom_call" | custom-call | flops 100000000 | bytes 100000 | tf_op jit(solution)/shard_map/pallas_call | solution.py:404
  2.3 1.4 %collective-permute-start.2 = (bf16[10,32,128]{2,1,0:T(8,128)(2,1)}, bf16[10,32,128]{2,1,0:T(8,128)(2,1)S(1)}, u32[]{:S(2)}, u32[]{:S(2)}) collective-permute-start(bf16[10,32,128]{2,1,0:T(8,128)(2,1)} %shard_map.120.own), channel_id=1, source_target_pairs={{16,0},{32,16},{48,32},{64,48},{80,64},{96,80},{112,96},{128,112},... | collective-permute-start | bytes 245768 | tf_op jit(solution)/shard_map/ppermute | solution.py:418
  3.7 6.3 %collective-permute-start.1 = (bf16[10,32,128]{2,1,0:T(8,128)(2,1)}, bf16[10,32,128]{2,1,0:T(8,128)(2,1)S(1)}, u32[]{:S(2)}, u32[]{:S(2)}) collective-permute-start(bf16[10,32,128]{2,1,0:T(8,128)(2,1)} %shard_map.120.own), channel_id=1, source_target_pairs={{0,16},{16,32},{32,48},{48,64},{64,80},{80,96},{96,112},{112,128},... | collective-permute-start | bytes 245768 | tf_op jit(solution)/shard_map/ppermute | solution.py:417
  10.0 0.9 slice.13
  10.9 1.3 %collective-permute-start.3 = (bf16[8,32,128]{2,1,0:T(8,128)(2,1)S(1)}, bf16[8,32,128]{2,1,0:T(8,128)(2,1)S(1)}, u32[]{:S(2)}, u32[]{:S(2)}) collective-permute-start(bf16[8,32,128]{2,1,0:T(8,128)(2,1)S(1)} %slice.13), channel_id=1, source_target_pairs={{32,0},{48,16},{64,32},{80,48},{96,64},{112,80},{128,96},{144,112}... | collective-permute-start | bytes 196616 | tf_op jit(solution)/shard_map/ppermute | solution.py:418
  12.2 4.2 %collective-permute-start = (bf16[8,32,128]{2,1,0:T(8,128)(2,1)S(1)}, bf16[8,32,128]{2,1,0:T(8,128)(2,1)S(1)}, u32[]{:S(2)}, u32[]{:S(2)}) collective-permute-start(bf16[8,32,128]{2,1,0:T(8,128)(2,1)S(1)} %slice.13), channel_id=1, source_target_pairs={{0,32},{16,48},{32,64},{48,80},{64,96},{80,112},{96,128},{112,144}... | collective-permute-start | bytes 196616 | tf_op jit(solution)/shard_map/ppermute | solution.py:417
  16.4 1.3 %collective-permute-done.far_prev = bf16[8,32,128]{2,1,0:T(8,128)(2,1)S(1)} collective-permute-done((bf16[8,32,128]{2,1,0:T(8,128)(2,1)S(1)}, bf16[8,32,128]{2,1,0:T(8,128)(2,1)S(1)}, u32[]{:S(2)}, u32[]{:S(2)}) %collective-permute-start) | collective-permute-done | bytes 65568 | tf_op jit(solution)/shard_map/ppermute | solution.py:417
  17.7 0.9 copy-done
  18.6 0.7 copy-done.1
  19.3 0.8 shard_map.121
  20.1 9.5 %collective-permute-start.5 = (bf16[38,32,128]{2,1,0:T(8,128)(2,1)S(1)}, bf16[38,32,128]{2,1,0:T(8,128)(2,1)S(1)}, u32[]{:S(2)}, u32[]{:S(2)}) collective-permute-start(bf16[38,32,128]{2,1,0:T(8,128)(2,1)S(1)} %get-tuple-element.16), channel_id=1, source_target_pairs={{1,0},{2,1},{3,2},{4,3},{5,4},{6,5},{7,6},{8,7},{9,8},{10,9},{11,1... | collective-permute-start | bytes 933896 | tf_op jit(solution)/shard_map/ppermute | solution.py:418
  29.6 1.9 %collective-permute-start.4 = (bf16[38,32,128]{2,1,0:T(8,128)(2,1)S(1)}, bf16[38,32,128]{2,1,0:T(8,128)(2,1)S(1)}, u32[]{:S(2)}, u32[]{:S(2)}) collective-permute-start(bf16[38,32,128]{2,1,0:T(8,128)(2,1)S(1)} %get-tuple-element.16), channel_id=1, source_target_pairs={{0,1},{1,2},{2,3},{3,4},{4,5},{5,6},{6,7},{7,8},{8,9},{9,10},{10,1... | collective-permute-start | bytes 933896 | tf_op jit(solution)/shard_map/ppermute | solution.py:417
  31.5 0.8 reshape.34
  32.3 3.8 %all-to-all-start = ((bf16[16,40,128]{2,1,0:T(8,128)(2,1)}), bf16[16,40,128]{2,1,0:T(8,128)(2,1)S(1)}, u32[]{:S(2)}, u32[]{:S(2)}) async-start(bf16[16,40,128]{2,1,0:T(8,128)(2,1)} %get-tuple-element.18), calls=%async_computation | async-start | bytes 327680 | tf_op jit(solution)/shard_map/all_to_all | solution.py:450
  36.2 0.1 slice.14
  36.3 0.4 pad_maximum_fusion.refs_0_
  36.7 4.5 %shard_map.122 = (bf16[8,32,128]{2,1,0:T(8,128)(2,1)S(1)}, bf16[4,128,384]{2,1,0:T(8,128)(2,1)S(1)}, bf16[4,256,384]{2,1,0:T(8,128)(2,1)S(1)}, bf16[8,32,512]{2,1,0:T(8,128)(2,1)S(1)}, bf16[6,144,512]{2,1,0:T(8,128)(2,1)S(1)}) custom-call(bf16[38,96,128]{2,1,0:T(8,128)(2,1)S(1)} %pad_maximum_fusion.refs_0_, bf16[128,16]{1,0:T(8,128)(2,1)S(1)} %pad.4.refs_1_, ...), custom_call_target="tpu_custom_call" | custom-call | flops 5000000000 | bytes 100000 | tf_op jit(solution)/shard_map/pallas_call | solution.py:404
  41.2 0.9 copy-done.6
  42.1 0.8 copy-done.8
  42.9 0.7 copy-done.10
  43.6 2.1 %collective-permute-start.7 = (bf16[8,32,128]{2,1,0:T(8,128)(2,1)S(1)}, bf16[8,32,128]{2,1,0:T(8,128)(2,1)S(1)}, u32[]{:S(2)}, u32[]{:S(2)}) collective-permute-start(bf16[8,32,128]{2,1,0:T(8,128)(2,1)S(1)} %get-tuple-element.17.refs_1_), channel_id=1, source_target_pairs={{1,0},{2,1},{3,2},{4,3},{5,4},{6,5},{7,6},{8,7},{9,8},{10,9},{11,1... | collective-permute-start | bytes 196616 | tf_op jit(solution)/shard_map/ppermute | solution.py:418
  45.7 3.4 %collective-permute-start.6 = (bf16[8,32,128]{2,1,0:T(8,128)(2,1)S(1)}, bf16[8,32,128]{2,1,0:T(8,128)(2,1)S(1)}, u32[]{:S(2)}, u32[]{:S(2)}) collective-permute-start(bf16[8,32,128]{2,1,0:T(8,128)(2,1)S(1)} %get-tuple-element.17.refs_1_), channel_id=1, source_target_pairs={{0,1},{1,2},{2,3},{3,4},{4,5},{5,6},{6,7},{7,8},{8,9},{9,10},{10,1... | collective-permute-start | bytes 196616 | tf_op jit(solution)/shard_map/ppermute | solution.py:417
  49.1 1.3 %collective-permute-done.6.refs_0_ = bf16[8,32,128]{2,1,0:T(8,128)(2,1)S(1)} collective-permute-done((bf16[8,32,128]{2,1,0:T(8,128)(2,1)S(1)}, bf16[8,32,128]{2,1,0:T(8,128)(2,1)S(1)}, u32[]{:S(2)}, u32[]{:S(2)}) %collective-permute-start.6) | collective-permute-done | bytes 65568 | tf_op jit(solution)/shard_map/ppermute | solution.py:417
  50.4 1.1 copy-done.7
  51.6 1.0 copy-done.9
  52.6 0.9 copy-done.11
  53.5 6.5 %shard_map.123 = bf16[32,24,128]{2,1,0:T(8,128)(2,1)S(1)} custom-call(bf16[8,32,128]{2,1,0:T(8,128)(2,1)S(1)} %collective-permute-done.6.refs_0_, bf16[8,32,128]{2,1,0:T(8,128)(2,1)S(1)} %get-tuple-element.17.refs_1_, bf16[8,32,128]{2,1,0:T(8,128)(2,1)S(1)} %collective-permute-done.7.refs_2_, bf16[16,40,128]{2,1,0:T(8,128)(2,1)S(1)} %all-to-all-done.refs_3_, ...), custom_call_target="tpu_custom_call" | custom-call | flops 11000000512 | bytes 100000 | tf_op jit(solution)/shard_map/pallas_call | solution.py:404
  60.0 16.1 %all_to_all.20.got = bf16[32,24,128]{2,1,0:T(8,128)(2,1)S(1)} all-to-all(bf16[32,24,128]{2,1,0:T(8,128)(2,1)S(1)} %shard_map.123), channel_id=1, replica_groups={{0,1,2,3,4,5,6,7,8,9,10,11,12,13,14,15,16,17,18,19,20,21,22,23,24,25,26..., dimensions={0} | all-to-all | bytes 393216 | tf_op jit(solution)/shard_map/all_to_all | solution.py:478
  76.1 0.6 shard_map.124
  76.7 29.4 %all_to_all.21.got = bf16[16,24,128]{2,1,0:T(8,128)(2,1)S(1)} all-to-all(bf16[16,24,128]{2,1,0:T(8,128)(2,1)S(1)} %get-tuple-element.24), channel_id=1, replica_groups={{0,32,64,96,128,160,192,224,256,288,320,352,384,416,448,480},{16,48,80,..., dimensions={0} | all-to-all | bytes 196608 | tf_op jit(solution)/shard_map/all_to_all | solution.py:482
  106.2 13.9 %all_to_all.22.refs_0_ = bf16[32,24,128]{2,1,0:T(8,128)(2,1)S(1)} all-to-all(bf16[32,24,128]{2,1,0:T(8,128)(2,1)S(1)} %shard_map.125), channel_id=1, replica_groups={{0,1,2,3,4,5,6,7,8,9,10,11,12,13,14,15,16,17,18,19,20,21,22,23,24,25,26..., dimensions={0} | all-to-all | bytes 393216 | tf_op jit(solution)/shard_map/all_to_all | solution.py:484
  120.1 0.9 shard_map.126
  (26 shorter events, 0.1 us)
Async XLA Ops:
  2.3 34.4 %copy-start.2 = (bf16[32,16,3,3,3]{0,1,4,3,2:T(8,128)(2,1)S(1)}, bf16[32,16,3,3,3]{0,1,4,3,2:T(8,128)(2,1)}, u32[]{:S(2)}) copy-start(bf16[32,16,3,3,3]{0,1,4,3,2:T(8,128)(2,1)} %param.11) | copy-start | bytes 82948
  2.3 15.4 %collective-permute-start.2 = (bf16[10,32,128]{2,1,0:T(8,128)(2,1)}, bf16[10,32,128]{2,1,0:T(8,128)(2,1)S(1)}, u32[]{:S(2)}, u32[]{:S(2)}) collective-permute-start(bf16[10,32,128]{2,1,0:T(8,128)(2,1)} %shard_map.120.own), channel_id=1, source_target_pairs={{16,0},{32,16},{48,32},{64,48},{80,64},{96,80},{112,96},{128,112},... | collective-permute-start | bytes 245768 | tf_op jit(solution)/shard_map/ppermute | solution.py:418
  3.7 14.0 %collective-permute-start.1 = (bf16[10,32,128]{2,1,0:T(8,128)(2,1)}, bf16[10,32,128]{2,1,0:T(8,128)(2,1)S(1)}, u32[]{:S(2)}, u32[]{:S(2)}) collective-permute-start(bf16[10,32,128]{2,1,0:T(8,128)(2,1)} %shard_map.120.own), channel_id=1, source_target_pairs={{0,16},{16,32},{32,48},{48,64},{64,80},{80,96},{96,112},{112,128},... | collective-permute-start | bytes 245768 | tf_op jit(solution)/shard_map/ppermute | solution.py:417
  10.9 5.5 %collective-permute-start.3 = (bf16[8,32,128]{2,1,0:T(8,128)(2,1)S(1)}, bf16[8,32,128]{2,1,0:T(8,128)(2,1)S(1)}, u32[]{:S(2)}, u32[]{:S(2)}) collective-permute-start(bf16[8,32,128]{2,1,0:T(8,128)(2,1)S(1)} %slice.13), channel_id=1, source_target_pairs={{32,0},{48,16},{64,32},{80,48},{96,64},{112,80},{128,96},{144,112}... | collective-permute-start | bytes 196616 | tf_op jit(solution)/shard_map/ppermute | solution.py:418
  12.2 5.5 %collective-permute-start = (bf16[8,32,128]{2,1,0:T(8,128)(2,1)S(1)}, bf16[8,32,128]{2,1,0:T(8,128)(2,1)S(1)}, u32[]{:S(2)}, u32[]{:S(2)}) collective-permute-start(bf16[8,32,128]{2,1,0:T(8,128)(2,1)S(1)} %slice.13), channel_id=1, source_target_pairs={{0,32},{16,48},{32,64},{48,80},{64,96},{80,112},{96,128},{112,144}... | collective-permute-start | bytes 196616 | tf_op jit(solution)/shard_map/ppermute | solution.py:417
  17.7 0.9 copy-start
  18.6 0.7 copy-start.1
  19.3 17.3 %copy-start.4 = (bf16[2048,128]{1,0:T(8,128)(2,1)S(1)}, bf16[2048,128]{1,0:T(8,128)(2,1)}, u32[]{:S(2)}) copy-start(bf16[2048,128]{1,0:T(8,128)(2,1)} %constant.11.clone.refs_3_.refs_9_) | copy-start | bytes 1572868
  20.1 16.0 %collective-permute-start.5 = (bf16[38,32,128]{2,1,0:T(8,128)(2,1)S(1)}, bf16[38,32,128]{2,1,0:T(8,128)(2,1)S(1)}, u32[]{:S(2)}, u32[]{:S(2)}) collective-permute-start(bf16[38,32,128]{2,1,0:T(8,128)(2,1)S(1)} %get-tuple-element.16), channel_id=1, source_target_pairs={{1,0},{2,1},{3,2},{4,3},{5,4},{6,5},{7,6},{8,7},{9,8},{10,9},{11,1... | collective-permute-start | bytes 933896 | tf_op jit(solution)/shard_map/ppermute | solution.py:418
  29.6 6.6 %collective-permute-start.4 = (bf16[38,32,128]{2,1,0:T(8,128)(2,1)S(1)}, bf16[38,32,128]{2,1,0:T(8,128)(2,1)S(1)}, u32[]{:S(2)}, u32[]{:S(2)}) collective-permute-start(bf16[38,32,128]{2,1,0:T(8,128)(2,1)S(1)} %get-tuple-element.16), channel_id=1, source_target_pairs={{0,1},{1,2},{2,3},{3,4},{4,5},{5,6},{6,7},{7,8},{8,9},{9,10},{10,1... | collective-permute-start | bytes 933896 | tf_op jit(solution)/shard_map/ppermute | solution.py:417
  32.3 16.8 %all-to-all-start = ((bf16[16,40,128]{2,1,0:T(8,128)(2,1)}), bf16[16,40,128]{2,1,0:T(8,128)(2,1)S(1)}, u32[]{:S(2)}, u32[]{:S(2)}) async-start(bf16[16,40,128]{2,1,0:T(8,128)(2,1)} %get-tuple-element.18), calls=%async_computation | async-start | bytes 327680 | tf_op jit(solution)/shard_map/all_to_all | solution.py:450
  36.7 13.8 %copy-start.3 = (bf16[256,2304]{1,0:T(8,128)(2,1)S(1)}, bf16[256,2304]{1,0:T(8,128)(2,1)}, u32[]{:S(2)}) copy-start(bf16[256,2304]{1,0:T(8,128)(2,1)} %constant.12.clone.refs_10_) | copy-start | bytes 3538948
  36.7 13.8 %copy-start.5 = (bf16[256,512]{1,0:T(8,128)(2,1)S(1)}, bf16[256,512]{1,0:T(8,128)(2,1)}, u32[]{:S(2)}) copy-start(bf16[256,512]{1,0:T(8,128)(2,1)} %constant.14.clone.refs_12_) | copy-start | bytes 786436
  41.2 0.9 copy-start.6
  42.1 0.8 copy-start.8
  42.9 0.7 copy-start.10
  43.6 5.6 %collective-permute-start.7 = (bf16[8,32,128]{2,1,0:T(8,128)(2,1)S(1)}, bf16[8,32,128]{2,1,0:T(8,128)(2,1)S(1)}, u32[]{:S(2)}, u32[]{:S(2)}) collective-permute-start(bf16[8,32,128]{2,1,0:T(8,128)(2,1)S(1)} %get-tuple-element.17.refs_1_), channel_id=1, source_target_pairs={{1,0},{2,1},{3,2},{4,3},{5,4},{6,5},{7,6},{8,7},{9,8},{10,9},{11,1... | collective-permute-start | bytes 196616 | tf_op jit(solution)/shard_map/ppermute | solution.py:418
  45.7 4.8 %collective-permute-start.6 = (bf16[8,32,128]{2,1,0:T(8,128)(2,1)S(1)}, bf16[8,32,128]{2,1,0:T(8,128)(2,1)S(1)}, u32[]{:S(2)}, u32[]{:S(2)}) collective-permute-start(bf16[8,32,128]{2,1,0:T(8,128)(2,1)S(1)} %get-tuple-element.17.refs_1_), channel_id=1, source_target_pairs={{0,1},{1,2},{2,3},{3,4},{4,5},{5,6},{6,7},{7,8},{8,9},{9,10},{10,1... | collective-permute-start | bytes 196616 | tf_op jit(solution)/shard_map/ppermute | solution.py:417
  50.4 1.1 copy-start.7
  51.6 1.0 copy-start.9
  52.6 0.9 copy-start.11

commit v2 on v1

--- a/solution.py
+++ b/solution.py
@@ -117,8 +117,8 @@
     return lax.broadcasted_iota(jnp.int32, (1, count), 1)
 
 
-def turned_field(volume_in, grads_in, field, volume, feature_grad, held, done):
-    pairs = ((volume_in, volume), (grads_in, feature_grad))
+def turned_field(volume_in, grads_in, weights_in, field, volume, feature_grad, w_third, held, done):
+    pairs = ((volume_in, volume), (grads_in, feature_grad), (weights_in, w_third))
     copies = [pltpu.make_async_copy(a, b, done.at[i]) for i, (a, b) in enumerate(pairs)]
     for copy in copies:
         copy.start()
@@ -131,7 +131,11 @@
             h = s + i - 1
             if 0 <= h < 16:
                 held[4 * s : 4 * s + 4, 16 * i : 16 * i + 16] = grads[:, h, :]
-    for t in range(2):
+    copies[2].wait()
+    for k in range(27):
+        g, i = divmod(k, 4)
+        held[64 + 4 * g : 68 + 4 * g, 32 * i : 32 * i + 32] = w_third[k].astype(F32)
+    for t in range(3):
         field[8 + t] = held[32 * t : 32 * t + 32].astype(BF16)
     copies[0].wait()
     for d in range(8):
@@ -139,7 +143,7 @@
         field[d] = dot(turn, stack.astype(BF16)).astype(BF16)
 
 
-def tall_field(w_third, far_prev, prev, own, nxt, far_nxt, tall, sent, held):
+def tall_field(far_prev, prev, own, nxt, far_nxt, tall, sent, held):
     for d in range(7):
         tall[d] = far_prev[d + 1]
         tall[31 + d] = far_nxt[d]
@@ -147,12 +151,9 @@
         tall[7 + d] = prev[d]
         tall[15 + d] = own[d]
         tall[23 + d] = nxt[d]
-    held[...] = jnp.zeros(held.shape, F32)
-    for k in range(27):
-        g, i = divmod(k, 4)
-        held[0, 4 * g : 4 * g + 4, 32 * i : 32 * i + 32] = w_third[k].astype(F32)
-    for s in range(1, 16):
-        held[s, 0:28] = held[0, 0:28]
+    weights = own[10].astype(F32)[0:28]
+    for s in range(16):
+        held[s, 0:28] = weights
     for j, part in enumerate((prev, own, nxt)):
         for t in range(2):
             grads = part[8 + t].astype(F32)
@@ -434,22 +435,23 @@
 
     (field,) = call(
         turned_field,
-        [((10, 32, 128), BF16)],
-        [((4, 8, 8, 128), BF16), ((4, 16, 16), BF16), ((64, 128), F32)],
-        volume, feature_grad.reshape(4, 16, 16),
-        space=pl.ANY, copies=2, limit=None,
+        [((11, 32, 128), BF16)],
+        [((4, 8, 8, 128), BF16), ((4, 16, 16), BF16), ((27, 4, 32), BF16), ((96, 128), F32)],
+        volume, feature_grad.reshape(4, 16, 16), third_w,
+        space=pl.ANY, copies=3, limit=None,
     )
     prev, nxt = exchanged(field, field, "sx")
-    far_prev, far_nxt = exchanged(field[:8], field[:8], "sx", 2)
+    far_prev, far_nxt = exchanged(field, field, "sx", 2)
     tall, sent = call(
         tall_field,
         [((38, 32, 128), BF16), ((16, 40, 128), BF16)],
         [((16, 40, 128), F32)],
-        third_w, far_prev, prev, field, nxt, far_nxt,
+        far_prev, prev, field, nxt, far_nxt,
     )
     got = lax.all_to_all(sent, "sy", 0, 0, tiled=True)
     prev, nxt = exchanged(tall, tall, "sy")
     field = jnp.concatenate([prev[:, 4:], tall, nxt, nxt[:, :4]], axis=1)
+    field, got = lax.optimization_barrier((field, got))
     second, mask_a, patch_a, mask_b, patch_b = call(
         lambda *refs: forward(n_sx, *refs),
         [

time: 122 us -> 117 us (0.959)
  local copies, waits for them, and re-layouts: 8.82 us -> 1.8 us
  waiting for transfers between devices: 2.61 us -> 8.38 us
  blocking collectives: 59.4 us -> 56.1 us
    unnamed x24 -> x10, local copies, waits for them, and re-layouts: 7.06 us -> 0.9 us
    all_to_all x1, waiting for transfers between devices: 0.01 us -> 5.24 us  [shards(): got = lax.all_to_all(sent, 'sy', 0, 0, tiled=True)]
    all_to_all x1, blocking collectives: 16.1 us -> 14 us  [shards(): lax.all_to_all(parts, both, 0, 0, tiled=True, axis_index_groups=planes)]
    all_to_all x1, blocking collectives: 29.4 us -> 28.1 us  [shards(): got = lax.all_to_all(total, 'sx', 0, 0, tiled=True, axis_index_groups=lines)]
  transfers between devices with their start and end apart: 9 -> 9, of which waited for: 2 -> 3; matrix products, arithmetic and copies ran while one was open for 2% -> 1% of each run, Pallas kernels for 4% -> 0%
where the time goes in v2:
time: 117 us; the launch traced here: 116 us
  blocking collectives  56.1 us (48%)
  starting transfers between devices  33.9 us (29%)
  Pallas kernels  15 us (13%)
  waiting for transfers between devices  8.38 us (7%)
  local copies, waits for them, and re-layouts  1.8 us (2%)
    all_to_all x1, blocking collectives, shards(): got = lax.all_to_all(total, 'sx', 0, 0, tiled=True, axis_index_groups=lines)  28.1 us
    ppermute x4, starting transfers between devices, exchanged(): lax.ppermute(to_next, axis, [(i, i + step) for i in range(ends)])  15.7 us
    pallas_call x7, Pallas kernels, call(): pl.pallas_call(body, out_shape=[jax.ShapeDtypeStruct(shape, dtype) for sh...  15 us
    ppermute x4, starting transfers between devices, exchanged(): lax.ppermute(to_prev, axis, [(i + step, i) for i in range(ends)])  14.4 us
    all_to_all x1, blocking collectives, shards(): lax.all_to_all(parts, both, 0, 0, tiled=True, axis_index_groups=planes)  14 us
    all_to_all x1, blocking collectives, shards(): lax.all_to_all(total, both, 0, 0, tiled=True, axis_index_groups=planes)  13.9 us
    all_to_all x1, waiting for transfers between devices, shards(): got = lax.all_to_all(sent, 'sy', 0, 0, tiled=True)  5.24 us
    all_to_all x1, starting transfers between devices, shards(): got = lax.all_to_all(sent, 'sy', 0, 0, tiled=True)  3.83 us
  transfers between devices with their start and end apart: 9, of which 3 were waited for; matrix products, arithmetic and copies ran while one was open for 1% of the time, Pallas kernels for 0%

profile of v2, /device:TPU:1, one launch (start us, length us, event | category | flops | bytes accessed | tf_op | source)
XLA Modules:
  0.0 116.3 jit_solution(3500161514909043806)
XLA Ops:
  0.6 0.0 copy-start.1
  0.6 1.8 %shard_map.120.own = bf16[11,32,128]{2,1,0:T(8,128)(2,1)} custom-call(bf16[4,8,8,128]{3,2,1,0:T(8,128)(2,1)} %volume_in.1, bf16[4,16,16]{2,1,0:T(8,128)(2,1)} %bitcast.24, bf16[27,4,32]{2,1,0:T(4,128)(2,1)} %bitcast.23), custom_call_target="tpu_custom_call" | custom-call | flops 100000000 | bytes 100000 | tf_op jit(solution)/shard_map/pallas_call | solution.py:405
  2.4 1.3 %collective-permute-start.3 = (bf16[11,32,128]{2,1,0:T(8,128)(2,1)}, bf16[11,32,128]{2,1,0:T(8,128)(2,1)S(1)}, u32[]{:S(2)}, u32[]{:S(2)}) collective-permute-start(bf16[11,32,128]{2,1,0:T(8,128)(2,1)} %shard_map.120.own), channel_id=1, source_target_pairs={{32,0},{48,16},{64,32},{80,48},{96,64},{112,80},{128,96},{144,112}... | collective-permute-start | bytes 270344 | tf_op jit(solution)/shard_map/ppermute | solution.py:419
  3.7 1.3 %collective-permute-start.2 = (bf16[11,32,128]{2,1,0:T(8,128)(2,1)}, bf16[11,32,128]{2,1,0:T(8,128)(2,1)S(1)}, u32[]{:S(2)}, u32[]{:S(2)}) collective-permute-start(bf16[11,32,128]{2,1,0:T(8,128)(2,1)} %shard_map.120.own), channel_id=1, source_target_pairs={{16,0},{32,16},{48,32},{64,48},{80,64},{96,80},{112,96},{128,112},... | collective-permute-start | bytes 270344 | tf_op jit(solution)/shard_map/ppermute | solution.py:419
  5.0 6.3 %collective-permute-start.1 = (bf16[11,32,128]{2,1,0:T(8,128)(2,1)}, bf16[11,32,128]{2,1,0:T(8,128)(2,1)S(1)}, u32[]{:S(2)}, u32[]{:S(2)}) collective-permute-start(bf16[11,32,128]{2,1,0:T(8,128)(2,1)} %shard_map.120.own), channel_id=1, source_target_pairs={{0,16},{16,32},{32,48},{48,64},{64,80},{80,96},{96,112},{112,128},... | collective-permute-start | bytes 270344 | tf_op jit(solution)/shard_map/ppermute | solution.py:418
  11.3 4.2 %collective-permute-start = (bf16[11,32,128]{2,1,0:T(8,128)(2,1)}, bf16[11,32,128]{2,1,0:T(8,128)(2,1)S(1)}, u32[]{:S(2)}, u32[]{:S(2)}) collective-permute-start(bf16[11,32,128]{2,1,0:T(8,128)(2,1)} %shard_map.120.own), channel_id=1, source_target_pairs={{0,32},{16,48},{32,64},{48,80},{64,96},{80,112},{96,128},{112,144}... | collective-permute-start | bytes 270344 | tf_op jit(solution)/shard_map/ppermute | solution.py:418
  15.5 0.0 collective-permute-done.3.far_nxt
  15.6 0.0 collective-permute-done.2.nxt
  15.6 0.0 collective-permute-done.1.prev
  15.6 1.8 %collective-permute-done.far_prev = bf16[11,32,128]{2,1,0:T(8,128)(2,1)S(1)} collective-permute-done((bf16[11,32,128]{2,1,0:T(8,128)(2,1)}, bf16[11,32,128]{2,1,0:T(8,128)(2,1)S(1)}, u32[]{:S(2)}, u32[]{:S(2)}) %collective-permute-start) | collective-permute-done | bytes 90144 | tf_op jit(solution)/shard_map/ppermute | solution.py:418
  17.4 0.9 copy-done
  18.3 0.7 shard_map.121
  19.0 9.5 %collective-permute-start.5 = (bf16[38,32,128]{2,1,0:T(8,128)(2,1)S(1)}, bf16[38,32,128]{2,1,0:T(8,128)(2,1)S(1)}, u32[]{:S(2)}, u32[]{:S(2)}) collective-permute-start(bf16[38,32,128]{2,1,0:T(8,128)(2,1)S(1)} %get-tuple-element.18), channel_id=1, source_target_pairs={{1,0},{2,1},{3,2},{4,3},{5,4},{6,5},{7,6},{8,7},{9,8},{10,9},{11,1... | collective-permute-start | bytes 933896 | tf_op jit(solution)/shard_map/ppermute | solution.py:419
  28.5 1.9 %collective-permute-start.4 = (bf16[38,32,128]{2,1,0:T(8,128)(2,1)S(1)}, bf16[38,32,128]{2,1,0:T(8,128)(2,1)S(1)}, u32[]{:S(2)}, u32[]{:S(2)}) collective-permute-start(bf16[38,32,128]{2,1,0:T(8,128)(2,1)S(1)} %get-tuple-element.18), channel_id=1, source_target_pairs={{0,1},{1,2},{2,3},{3,4},{4,5},{5,6},{6,7},{7,8},{8,9},{9,10},{10,1... | collective-permute-start | bytes 933896 | tf_op jit(solution)/shard_map/ppermute | solution.py:418
  30.4 3.8 %all-to-all-start = ((bf16[16,40,128]{2,1,0:T(8,128)(2,1)}), bf16[16,40,128]{2,1,0:T(8,128)(2,1)S(1)}, u32[]{:S(2)}, u32[]{:S(2)}) async-start(bf16[16,40,128]{2,1,0:T(8,128)(2,1)} %get-tuple-element.19), calls=%async_computation | async-start | bytes 327680 | tf_op jit(solution)/shard_map/all_to_all | solution.py:451
  34.2 0.8 reshape.34
  35.0 0.0 collective-permute-done.5
  35.1 0.0 collective-permute-done.4
  35.1 0.1 slice.8
  35.2 0.4 pad_maximum_fusion.refs_0_
  35.5 5.2 %all-to-all-done.refs_3_ = bf16[16,40,128]{2,1,0:T(8,128)(2,1)S(1)} async-done(((bf16[16,40,128]{2,1,0:T(8,128)(2,1)}), bf16[16,40,128]{2,1,0:T(8,128)(2,1)S(1)}, u32[]{:S(2)}, u32[]{:S(2)}) %all-to-all-start) | async-done | bytes 163872 | tf_op jit(solution)/shard_map/all_to_all | solution.py:451
  40.8 4.5 %shard_map.122 = (bf16[8,32,128]{2,1,0:T(8,128)(2,1)S(1)}, bf16[4,128,384]{2,1,0:T(8,128)(2,1)S(1)}, bf16[4,256,384]{2,1,0:T(8,128)(2,1)S(1)}, bf16[8,32,512]{2,1,0:T(8,128)(2,1)S(1)}, bf16[6,144,512]{2,1,0:T(8,128)(2,1)S(1)}) custom-call(bf16[38,96,128]{2,1,0:T(8,128)(2,1)S(1)} %pad_maximum_fusion.refs_0_, bf16[128,16]{1,0:T(8,128)(2,1)S(1)} %pad.4.refs_1_, ...), custom_call_target="tpu_custom_call" | custom-call | flops 5000000000 | bytes 100000 | tf_op jit(solution)/shard_map/pallas_call | solution.py:405
  45.3 2.3 %collective-permute-start.7 = (bf16[8,32,128]{2,1,0:T(8,128)(2,1)S(1)}, bf16[8,32,128]{2,1,0:T(8,128)(2,1)S(1)}, u32[]{:S(2)}, u32[]{:S(2)}) collective-permute-start(bf16[8,32,128]{2,1,0:T(8,128)(2,1)S(1)} %get-tuple-element.21.refs_1_), channel_id=1, source_target_pairs={{1,0},{2,1},{3,2},{4,3},{5,4},{6,5},{7,6},{8,7},{9,8},{10,9},{11,1... | collective-permute-start | bytes 196616 | tf_op jit(solution)/shard_map/ppermute | solution.py:419
  47.7 3.2 %collective-permute-start.6 = (bf16[8,32,128]{2,1,0:T(8,128)(2,1)S(1)}, bf16[8,32,128]{2,1,0:T(8,128)(2,1)S(1)}, u32[]{:S(2)}, u32[]{:S(2)}) collective-permute-start(bf16[8,32,128]{2,1,0:T(8,128)(2,1)S(1)} %get-tuple-element.21.refs_1_), channel_id=1, source_target_pairs={{0,1},{1,2},{2,3},{3,4},{4,5},{5,6},{6,7},{7,8},{8,9},{9,10},{10,1... | collective-permute-start | bytes 196616 | tf_op jit(solution)/shard_map/ppermute | solution.py:418
  50.9 0.0 collective-permute-done.7.refs_2_
  50.9 1.3 %collective-permute-done.6.refs_0_ = bf16[8,32,128]{2,1,0:T(8,128)(2,1)S(1)} collective-permute-done((bf16[8,32,128]{2,1,0:T(8,128)(2,1)S(1)}, bf16[8,32,128]{2,1,0:T(8,128)(2,1)S(1)}, u32[]{:S(2)}, u32[]{:S(2)}) %collective-permute-start.6) | collective-permute-done | bytes 65568 | tf_op jit(solution)/shard_map/ppermute | solution.py:418
  52.2 6.4 %shard_map.123 = bf16[32,24,128]{2,1,0:T(8,128)(2,1)S(1)} custom-call(bf16[8,32,128]{2,1,0:T(8,128)(2,1)S(1)} %collective-permute-done.6.refs_0_, bf16[8,32,128]{2,1,0:T(8,128)(2,1)S(1)} %get-tuple-element.21.refs_1_, bf16[8,32,128]{2,1,0:T(8,128)(2,1)S(1)} %collective-permute-done.7.refs_2_, bf16[16,40,128]{2,1,0:T(8,128)(2,1)S(1)} %all-to-all-done.refs_3_, ...), custom_call_target="tpu_custom_call" | custom-call | flops 11000000512 | bytes 100000 | tf_op jit(solution)/shard_map/pallas_call | solution.py:405
  58.7 14.0 %all_to_all.20.got = bf16[32,24,128]{2,1,0:T(8,128)(2,1)S(1)} all-to-all(bf16[32,24,128]{2,1,0:T(8,128)(2,1)S(1)} %shard_map.123), channel_id=1, replica_groups={{0,1,2,3,4,5,6,7,8,9,10,11,12,13,14,15,16,17,18,19,20,21,22,23,24,25,26..., dimensions={0} | all-to-all | bytes 393216 | tf_op jit(solution)/shard_map/all_to_all | solution.py:480
  72.7 0.6 shard_map.124
  73.3 28.1 %all_to_all.21.got = bf16[16,24,128]{2,1,0:T(8,128)(2,1)S(1)} all-to-all(bf16[16,24,128]{2,1,0:T(8,128)(2,1)S(1)} %get-tuple-element.28), channel_id=1, replica_groups={{0,32,64,96,128,160,192,224,256,288,320,352,384,416,448,480},{16,48,80,..., dimensions={0} | all-to-all | bytes 196608 | tf_op jit(solution)/shard_map/all_to_all | solution.py:484
  101.5 13.9 %all_to_all.22.refs_0_ = bf16[32,24,128]{2,1,0:T(8,128)(2,1)S(1)} all-to-all(bf16[32,24,128]{2,1,0:T(8,128)(2,1)S(1)} %shard_map.125), channel_id=1, replica_groups={{0,1,2,3,4,5,6,7,8,9,10,11,12,13,14,15,16,17,18,19,20,21,22,23,24,25,26..., dimensions={0} | all-to-all | bytes 393216 | tf_op jit(solution)/shard_map/all_to_all | solution.py:486
  115.4 0.9 shard_map.126
  (11 shorter events, 0.1 us)
Async XLA Ops:
  0.6 40.1 %copy-start.1 = (bf16[32,16,3,3,3]{0,1,4,3,2:T(8,128)(2,1)S(1)}, bf16[32,16,3,3,3]{0,1,4,3,2:T(8,128)(2,1)}, u32[]{:S(2)}) copy-start(bf16[32,16,3,3,3]{0,1,4,3,2:T(8,128)(2,1)} %param.11) | copy-start | bytes 82948
  2.4 13.1 %collective-permute-start.3 = (bf16[11,32,128]{2,1,0:T(8,128)(2,1)}, bf16[11,32,128]{2,1,0:T(8,128)(2,1)S(1)}, u32[]{:S(2)}, u32[]{:S(2)}) collective-permute-start(bf16[11,32,128]{2,1,0:T(8,128)(2,1)} %shard_map.120.own), channel_id=1, source_target_pairs={{32,0},{48,16},{64,32},{80,48},{96,64},{112,80},{128,96},{144,112}... | collective-permute-start | bytes 270344 | tf_op jit(solution)/shard_map/ppermute | solution.py:419
  3.7 11.8 %collective-permute-start.2 = (bf16[11,32,128]{2,1,0:T(8,128)(2,1)}, bf16[11,32,128]{2,1,0:T(8,128)(2,1)S(1)}, u32[]{:S(2)}, u32[]{:S(2)}) collective-permute-start(bf16[11,32,128]{2,1,0:T(8,128)(2,1)} %shard_map.120.own), channel_id=1, source_target_pairs={{16,0},{32,16},{48,32},{64,48},{80,64},{96,80},{112,96},{128,112},... | collective-permute-start | bytes 270344 | tf_op jit(solution)/shard_map/ppermute | solution.py:419
  5.0 10.5 %collective-permute-start.1 = (bf16[11,32,128]{2,1,0:T(8,128)(2,1)}, bf16[11,32,128]{2,1,0:T(8,128)(2,1)S(1)}, u32[]{:S(2)}, u32[]{:S(2)}) collective-permute-start(bf16[11,32,128]{2,1,0:T(8,128)(2,1)} %shard_map.120.own), channel_id=1, source_target_pairs={{0,16},{16,32},{32,48},{48,64},{64,80},{80,96},{96,112},{112,128},... | collective-permute-start | bytes 270344 | tf_op jit(solution)/shard_map/ppermute | solution.py:418
  11.3 6.1 %collective-permute-start = (bf16[11,32,128]{2,1,0:T(8,128)(2,1)}, bf16[11,32,128]{2,1,0:T(8,128)(2,1)S(1)}, u32[]{:S(2)}, u32[]{:S(2)}) collective-permute-start(bf16[11,32,128]{2,1,0:T(8,128)(2,1)} %shard_map.120.own), channel_id=1, source_target_pairs={{0,32},{16,48},{32,64},{48,80},{64,96},{80,112},{96,128},{112,144}... | collective-permute-start | bytes 270344 | tf_op jit(solution)/shard_map/ppermute | solution.py:418
  17.4 0.9 copy-start
  18.3 22.5 %copy-start.3 = (bf16[2048,128]{1,0:T(8,128)(2,1)S(1)}, bf16[2048,128]{1,0:T(8,128)(2,1)}, u32[]{:S(2)}) copy-start(bf16[2048,128]{1,0:T(8,128)(2,1)} %constant.11.clone.refs_3_.refs_9_) | copy-start | bytes 1572868
  19.0 16.0 %collective-permute-start.5 = (bf16[38,32,128]{2,1,0:T(8,128)(2,1)S(1)}, bf16[38,32,128]{2,1,0:T(8,128)(2,1)S(1)}, u32[]{:S(2)}, u32[]{:S(2)}) collective-permute-start(bf16[38,32,128]{2,1,0:T(8,128)(2,1)S(1)} %get-tuple-element.18), channel_id=1, source_target_pairs={{1,0},{2,1},{3,2},{4,3},{5,4},{6,5},{7,6},{8,7},{9,8},{10,9},{11,1... | collective-permute-start | bytes 933896 | tf_op jit(solution)/shard_map/ppermute | solution.py:419
  28.5 6.6 %collective-permute-start.4 = (bf16[38,32,128]{2,1,0:T(8,128)(2,1)S(1)}, bf16[38,32,128]{2,1,0:T(8,128)(2,1)S(1)}, u32[]{:S(2)}, u32[]{:S(2)}) collective-permute-start(bf16[38,32,128]{2,1,0:T(8,128)(2,1)S(1)} %get-tuple-element.18), channel_id=1, source_target_pairs={{0,1},{1,2},{2,3},{3,4},{4,5},{5,6},{6,7},{7,8},{8,9},{9,10},{10,1... | collective-permute-start | bytes 933896 | tf_op jit(solution)/shard_map/ppermute | solution.py:418
  30.4 10.4 %all-to-all-start = ((bf16[16,40,128]{2,1,0:T(8,128)(2,1)}), bf16[16,40,128]{2,1,0:T(8,128)(2,1)S(1)}, u32[]{:S(2)}, u32[]{:S(2)}) async-start(bf16[16,40,128]{2,1,0:T(8,128)(2,1)} %get-tuple-element.19), calls=%async_computation | async-start | bytes 327680 | tf_op jit(solution)/shard_map/all_to_all | solution.py:451
  40.8 11.4 %copy-start.2 = (bf16[256,2304]{1,0:T(8,128)(2,1)S(1)}, bf16[256,2304]{1,0:T(8,128)(2,1)}, u32[]{:S(2)}) copy-start(bf16[256,2304]{1,0:T(8,128)(2,1)} %constant.12.clone.refs_10_) | copy-start | bytes 3538948
  40.8 11.4 %copy-start.4 = (bf16[256,512]{1,0:T(8,128)(2,1)S(1)}, bf16[256,512]{1,0:T(8,128)(2,1)}, u32[]{:S(2)}) copy-start(bf16[256,512]{1,0:T(8,128)(2,1)} %constant.14.clone.refs_12_) | copy-start | bytes 786436
  45.3 5.6 %collective-permute-start.7 = (bf16[8,32,128]{2,1,0:T(8,128)(2,1)S(1)}, bf16[8,32,128]{2,1,0:T(8,128)(2,1)S(1)}, u32[]{:S(2)}, u32[]{:S(2)}) collective-permute-start(bf16[8,32,128]{2,1,0:T(8,128)(2,1)S(1)} %get-tuple-element.21.refs_1_), channel_id=1, source_target_pairs={{1,0},{2,1},{3,2},{4,3},{5,4},{6,5},{7,6},{8,7},{9,8},{10,9},{11,1... | collective-permute-start | bytes 196616 | tf_op jit(solution)/shard_map/ppermute | solution.py:419
  47.7 4.6 %collective-permute-start.6 = (bf16[8,32,128]{2,1,0:T(8,128)(2,1)S(1)}, bf16[8,32,128]{2,1,0:T(8,128)(2,1)S(1)}, u32[]{:S(2)}, u32[]{:S(2)}) collective-permute-start(bf16[8,32,128]{2,1,0:T(8,128)(2,1)S(1)} %get-tuple-element.21.refs_1_), channel_id=1, source_target_pairs={{0,1},{1,2},{2,3},{3,4},{4,5},{5,6},{6,7},{7,8},{8,9},{9,10},{10,1... | collective-permute-start | bytes 196616 | tf_op jit(solution)/shard_map/ppermute | solution.py:418

commit v3 on v2

--- a/solution.py
+++ b/solution.py
@@ -338,17 +338,22 @@
         )
     third_wg = jnp.concatenate([third_wg, jnp.zeros((64, 32), F32)], axis=1)
     second_wg = jnp.concatenate([second_wg, jnp.zeros((32, 80), F32)], axis=1)
-    held[...] = jnp.zeros(held.shape, F32)
+    tails = third_wg[:, 768:896]
+    early, late = pltpu.roll(features, 96, 1), pltpu.roll(features, 112, 1)
+    second_tail, first_low = second_wg[:, 384:512], pltpu.roll(first_wg, 64, 1)
     for q in range(32):
         hi, s = divmod(q, 16)
-        for g in range(7):
-            o = 4 * s + 2 * hi
-            held[q, 2 * g : 2 * g + 2] = third_wg[o : o + 2, 128 * g : 128 * g + 128]
-        for g in range(4):
-            held[q, 14 + g : 15 + g] = second_wg[q : q + 1, 128 * g : 128 * g + 128]
-        if hi == 0:
-            held[q, 18:19] = first_wg[s : s + 1]
-        held[q, 19:23] = features[4 * s : 4 * s + 4]
+        for j in range(2):
+            o, f = 4 * s + 2 * hi + j, 4 * s + 2 * j
+            for g in range(6):
+                held[q, j : j + 1, 128 * g : 128 * g + 128] = third_wg[o : o + 1, 128 * g : 128 * g + 128]
+            tail = tails[o : o + 1] + early[f : f + 1] + late[f + 1 : f + 2]
+            held[q, j : j + 1, 768:896] = tail
+        held[q, 0:1, 896:1024] = second_wg[q : q + 1, 0:128]
+        held[q, 1:2, 896:1024] = second_wg[q : q + 1, 128:256]
+        held[q, 0:1, 1024:1152] = second_wg[q : q + 1, 256:384]
+        half = (first_low if hi == 0 else first_wg)[s : s + 1]
+        held[q, 1:2, 1024:1152] = jnp.where(left, second_tail[q : q + 1], half)
     parts[...] = held[...].astype(BF16)
 
 
@@ -371,7 +376,8 @@
     arrived = got[pl.ds(16 * hi, 16)].astype(F32)
     for o in range(4):
         for s in range(16):
-            held[o, s : s + 1] = arrived[s, 19 + o : 20 + o, 0:16]
+            at = 864 + 16 * (o % 2)
+            held[o, s : s + 1] = arrived[s, o // 2 : o // 2 + 1, at : at + 16]
     features[...] = held[...].astype(BF16)
 
 
@@ -380,15 +386,17 @@
     held_b[...] = jnp.zeros(held_b.shape, F32)
     for q in range(32):
         part = got[q].astype(F32)
-        if q < 16:
-            held_a[q : q + 1] = part[18:19]
-        for g in range(4):
-            held_b[q : q + 1, 128 * g : 128 * g + 128] = part[14 + g : 15 + g]
+        held_b[q : q + 1, 0:128] = part[0:1, 896:1024]
+        held_b[q : q + 1, 128:256] = part[1:2, 896:1024]
+        held_b[q : q + 1, 256:384] = part[0:1, 1024:1152]
+        held_b[q : q + 1, 384:512] = part[1:2, 1024:1152]
+    left = lanes(128) < 64
+    low = pltpu.roll(held_b[0:16, 384:512], 64, 1)
+    held_a[0:16] = jnp.where(left, low, held_b[16:32, 384:512])
     for hi in range(2):
         part = scale_c * got[16 * hi + lax.axis_index("sy")].astype(F32)
         for k in range(27):
-            g, i = divmod(k, 4)
-            third[k, 2 * hi : 2 * hi + 2] = part[2 * g : 2 * g + 2, 32 * i : 32 * i + 32]
+            third[k, 2 * hi : 2 * hi + 2] = part[:, 32 * k : 32 * k + 32]
     turned_a = scale_a * jnp.transpose(held_a[...])
     for k in range(27):
         first[k] = turned_a[4 * k : 4 * k + 4, 0:16]
@@ -464,11 +472,11 @@
     prev, nxt = exchanged(second, second, "sy")
     (parts,) = call(
         lambda *refs: backward(n_sx, *refs),
-        [((32, 24, 128), BF16)],
+        [((32, 2, 1152), BF16)],
         [
             ((64, 896), F32), ((3, 64, 128), F32), ((8, 288, 256), BF16), ((6, 64, 256), BF16),
             ((6, 576, 256), BF16), ((1728, 32), F32), ((16, 896), F32),
-            ((6, 32, 512), BF16), ((6, 288, 256), BF16), ((32, 24, 128), F32),
+            ((6, 32, 512), BF16), ((6, 288, 256), BF16), ((32, 2, 1152), F32),
         ],
         prev, second, nxt, got, mask_a, patch_a, mask_b, patch_b, second_w, taps,
         table(tap_shift(8, 32, 0, 8)), table(tap_shift(8, 64, 2, 4)),
@@ -479,10 +487,10 @@
     both = ("sx", "sy")
     got = lax.all_to_all(parts, both, 0, 0, tiled=True, axis_index_groups=planes)
     total, features = call(
-        plane_sum, [((n_z, 24, 128), BF16), ((4, 16, 16), BF16)], [((4, 16, 16), F32)], got
+        plane_sum, [((n_z, 2, 1152), BF16), ((4, 16, 16), BF16)], [((4, 16, 16), F32)], got
     )
     got = lax.all_to_all(total, "sx", 0, 0, tiled=True, axis_index_groups=lines)
-    (total,) = call(spread_sum, [((32, 24, 128), BF16)], [], got)
+    (total,) = call(spread_sum, [((32, 2, 1152), BF16)], [], got)
     got = lax.all_to_all(total, both, 0, 0, tiled=True, axis_index_groups=planes)
     scales = (64.0 / math.sqrt(cells), 8.0 / math.sqrt(cells / 8), 1.0 / math.sqrt(cells / 64))
     first, second, third = call(

time: 117 us -> 116 us (level)
  blocking collectives: 56.1 us -> 54.8 us
where the time goes in v3:
time: 116 us; the launch traced here: 115 us
  blocking collectives  54.8 us (47%)
  starting transfers between devices  33.9 us (29%)
  Pallas kernels  15.3 us (13%)
  waiting for transfers between devices  8.38 us (7%)
  local copies, waits for them, and re-layouts  1.8 us (2%)
    all_to_all x1, blocking collectives, shards(): got = lax.all_to_all(total, 'sx', 0, 0, tiled=True, axis_index_groups=lines)  28 us
    ppermute x4, starting transfers between devices, exchanged(): lax.ppermute(to_next, axis, [(i, i + step) for i in range(ends)])  15.7 us
    pallas_call x7, Pallas kernels, call(): pl.pallas_call(body, out_shape=[jax.ShapeDtypeStruct(shape, dtype) for sh...  15.3 us
    ppermute x4, starting transfers between devices, exchanged(): lax.ppermute(to_prev, axis, [(i + step, i) for i in range(ends)])  14.4 us
    all_to_all x1, blocking collectives, shards(): lax.all_to_all(parts, both, 0, 0, tiled=True, axis_index_groups=planes)  13.7 us
    all_to_all x1, blocking collectives, shards(): lax.all_to_all(total, both, 0, 0, tiled=True, axis_index_groups=planes)  13.1 us
    all_to_all x1, waiting for transfers between devices, shards(): got = lax.all_to_all(sent, 'sy', 0, 0, tiled=True)  5.24 us
    all_to_all x1, starting transfers between devices, shards(): got = lax.all_to_all(sent, 'sy', 0, 0, tiled=True)  3.83 us
  transfers between devices with their start and end apart: 9, of which 3 were waited for; matrix products, arithmetic and copies ran while one was open for 1% of the time, Pallas kernels for 0%

profile of v3, /device:TPU:1, one launch (start us, length us, event | category | flops | bytes accessed | tf_op | source)
XLA Modules:
  0.0 115.3 jit_solution(4969957755697298886)
XLA Ops:
  0.6 1.8 %shard_map.120.own = bf16[11,32,128]{2,1,0:T(8,128)(2,1)} custom-call(bf16[4,8,8,128]{3,2,1,0:T(8,128)(2,1)} %volume_in.1, bf16[4,16,16]{2,1,0:T(8,128)(2,1)} %bitcast.24, bf16[27,4,32]{2,1,0:T(4,128)(2,1)} %bitcast.23), custom_call_target="tpu_custom_call" | custom-call | flops 100000000 | bytes 100000 | tf_op jit(solution)/shard_map/pallas_call | solution.py:413
  2.4 1.3 %collective-permute-start.3 = (bf16[11,32,128]{2,1,0:T(8,128)(2,1)}, bf16[11,32,128]{2,1,0:T(8,128)(2,1)S(1)}, u32[]{:S(2)}, u32[]{:S(2)}) collective-permute-start(bf16[11,32,128]{2,1,0:T(8,128)(2,1)} %shard_map.120.own), channel_id=1, source_target_pairs={{32,0},{48,16},{64,32},{80,48},{96,64},{112,80},{128,96},{144,112}... | collective-permute-start | bytes 270344 | tf_op jit(solution)/shard_map/ppermute | solution.py:427
  3.7 1.3 %collective-permute-start.2 = (bf16[11,32,128]{2,1,0:T(8,128)(2,1)}, bf16[11,32,128]{2,1,0:T(8,128)(2,1)S(1)}, u32[]{:S(2)}, u32[]{:S(2)}) collective-permute-start(bf16[11,32,128]{2,1,0:T(8,128)(2,1)} %shard_map.120.own), channel_id=1, source_target_pairs={{16,0},{32,16},{48,32},{64,48},{80,64},{96,80},{112,96},{128,112},... | collective-permute-start | bytes 270344 | tf_op jit(solution)/shard_map/ppermute | solution.py:427
  5.0 6.3 %collective-permute-start.1 = (bf16[11,32,128]{2,1,0:T(8,128)(2,1)}, bf16[11,32,128]{2,1,0:T(8,128)(2,1)S(1)}, u32[]{:S(2)}, u32[]{:S(2)}) collective-permute-start(bf16[11,32,128]{2,1,0:T(8,128)(2,1)} %shard_map.120.own), channel_id=1, source_target_pairs={{0,16},{16,32},{32,48},{48,64},{64,80},{80,96},{96,112},{112,128},... | collective-permute-start | bytes 270344 | tf_op jit(solution)/shard_map/ppermute | solution.py:426
  11.3 4.2 %collective-permute-start = (bf16[11,32,128]{2,1,0:T(8,128)(2,1)}, bf16[11,32,128]{2,1,0:T(8,128)(2,1)S(1)}, u32[]{:S(2)}, u32[]{:S(2)}) collective-permute-start(bf16[11,32,128]{2,1,0:T(8,128)(2,1)} %shard_map.120.own), channel_id=1, source_target_pairs={{0,32},{16,48},{32,64},{48,80},{64,96},{80,112},{96,128},{112,144}... | collective-permute-start | bytes 270344 | tf_op jit(solution)/shard_map/ppermute | solution.py:426
  15.5 0.0 collective-permute-done.3.far_nxt
  15.6 0.0 collective-permute-done.2.nxt
  15.6 0.0 collective-permute-done.1.prev
  15.6 1.8 %collective-permute-done.far_prev = bf16[11,32,128]{2,1,0:T(8,128)(2,1)S(1)} collective-permute-done((bf16[11,32,128]{2,1,0:T(8,128)(2,1)}, bf16[11,32,128]{2,1,0:T(8,128)(2,1)S(1)}, u32[]{:S(2)}, u32[]{:S(2)}) %collective-permute-start) | collective-permute-done | bytes 90144 | tf_op jit(solution)/shard_map/ppermute | solution.py:426
  17.4 0.9 copy-done
  18.3 0.7 shard_map.121
  19.0 9.5 %collective-permute-start.5 = (bf16[38,32,128]{2,1,0:T(8,128)(2,1)S(1)}, bf16[38,32,128]{2,1,0:T(8,128)(2,1)S(1)}, u32[]{:S(2)}, u32[]{:S(2)}) collective-permute-start(bf16[38,32,128]{2,1,0:T(8,128)(2,1)S(1)} %get-tuple-element.18), channel_id=1, source_target_pairs={{1,0},{2,1},{3,2},{4,3},{5,4},{6,5},{7,6},{8,7},{9,8},{10,9},{11,1... | collective-permute-start | bytes 933896 | tf_op jit(solution)/shard_map/ppermute | solution.py:427
  28.5 1.9 %collective-permute-start.4 = (bf16[38,32,128]{2,1,0:T(8,128)(2,1)S(1)}, bf16[38,32,128]{2,1,0:T(8,128)(2,1)S(1)}, u32[]{:S(2)}, u32[]{:S(2)}) collective-permute-start(bf16[38,32,128]{2,1,0:T(8,128)(2,1)S(1)} %get-tuple-element.18), channel_id=1, source_target_pairs={{0,1},{1,2},{2,3},{3,4},{4,5},{5,6},{6,7},{7,8},{8,9},{9,10},{10,1... | collective-permute-start | bytes 933896 | tf_op jit(solution)/shard_map/ppermute | solution.py:426
  30.4 3.8 %all-to-all-start = ((bf16[16,40,128]{2,1,0:T(8,128)(2,1)}), bf16[16,40,128]{2,1,0:T(8,128)(2,1)S(1)}, u32[]{:S(2)}, u32[]{:S(2)}) async-start(bf16[16,40,128]{2,1,0:T(8,128)(2,1)} %get-tuple-element.19), calls=%async_computation | async-start | bytes 327680 | tf_op jit(solution)/shard_map/all_to_all | solution.py:459
  34.2 0.8 reshape.34
  35.0 0.0 collective-permute-done.5
  35.1 0.0 collective-permute-done.4
  35.1 0.1 slice.8
  35.2 0.4 pad_maximum_fusion.refs_0_
  35.5 5.2 %all-to-all-done.refs_3_ = bf16[16,40,128]{2,1,0:T(8,128)(2,1)S(1)} async-done(((bf16[16,40,128]{2,1,0:T(8,128)(2,1)}), bf16[16,40,128]{2,1,0:T(8,128)(2,1)S(1)}, u32[]{:S(2)}, u32[]{:S(2)}) %all-to-all-start) | async-done | bytes 163872 | tf_op jit(solution)/shard_map/all_to_all | solution.py:459
  40.8 4.5 %shard_map.122 = (bf16[8,32,128]{2,1,0:T(8,128)(2,1)S(1)}, bf16[4,128,384]{2,1,0:T(8,128)(2,1)S(1)}, bf16[4,256,384]{2,1,0:T(8,128)(2,1)S(1)}, bf16[8,32,512]{2,1,0:T(8,128)(2,1)S(1)}, bf16[6,144,512]{2,1,0:T(8,128)(2,1)S(1)}) custom-call(bf16[38,96,128]{2,1,0:T(8,128)(2,1)S(1)} %pad_maximum_fusion.refs_0_, bf16[128,16]{1,0:T(8,128)(2,1)S(1)} %pad.4.refs_1_, ...), custom_call_target="tpu_custom_call" | custom-call | flops 5000000000 | bytes 100000 | tf_op jit(solution)/shard_map/pallas_call | solution.py:413
  45.3 2.3 %collective-permute-start.7 = (bf16[8,32,128]{2,1,0:T(8,128)(2,1)S(1)}, bf16[8,32,128]{2,1,0:T(8,128)(2,1)S(1)}, u32[]{:S(2)}, u32[]{:S(2)}) collective-permute-start(bf16[8,32,128]{2,1,0:T(8,128)(2,1)S(1)} %get-tuple-element.21.refs_1_), channel_id=1, source_target_pairs={{1,0},{2,1},{3,2},{4,3},{5,4},{6,5},{7,6},{8,7},{9,8},{10,9},{11,1... | collective-permute-start | bytes 196616 | tf_op jit(solution)/shard_map/ppermute | solution.py:427
  47.7 3.2 %collective-permute-start.6 = (bf16[8,32,128]{2,1,0:T(8,128)(2,1)S(1)}, bf16[8,32,128]{2,1,0:T(8,128)(2,1)S(1)}, u32[]{:S(2)}, u32[]{:S(2)}) collective-permute-start(bf16[8,32,128]{2,1,0:T(8,128)(2,1)S(1)} %get-tuple-element.21.refs_1_), channel_id=1, source_target_pairs={{0,1},{1,2},{2,3},{3,4},{4,5},{5,6},{6,7},{7,8},{8,9},{9,10},{10,1... | collective-permute-start | bytes 196616 | tf_op jit(solution)/shard_map/ppermute | solution.py:426
  50.9 0.0 collective-permute-done.7.refs_2_
  50.9 1.3 %collective-permute-done.6.refs_0_ = bf16[8,32,128]{2,1,0:T(8,128)(2,1)S(1)} collective-permute-done((bf16[8,32,128]{2,1,0:T(8,128)(2,1)S(1)}, bf16[8,32,128]{2,1,0:T(8,128)(2,1)S(1)}, u32[]{:S(2)}, u32[]{:S(2)}) %collective-permute-start.6) | collective-permute-done | bytes 65568 | tf_op jit(solution)/shard_map/ppermute | solution.py:426
  52.2 0.0 copy-done.2
  52.2 6.5 %shard_map.123 = bf16[32,2,1152]{2,1,0:T(2,128)(2,1)S(1)} custom-call(bf16[8,32,128]{2,1,0:T(8,128)(2,1)S(1)} %collective-permute-done.6.refs_0_, bf16[8,32,128]{2,1,0:T(8,128)(2,1)S(1)} %get-tuple-element.21.refs_1_, bf16[8,32,128]{2,1,0:T(8,128)(2,1)S(1)} %collective-permute-done.7.refs_2_, bf16[16,40,128]{2,1,0:T(8,128)(2,1)S(1)} %all-to-all-done.refs_3_, ...), custom_call_target="tpu_custom_call" | custom-call | flops 11000000512 | bytes 100000 | tf_op jit(solution)/shard_map/pallas_call | solution.py:413
  58.8 13.7 %all_to_all.20.got = bf16[32,2,1152]{2,1,0:T(2,128)(2,1)S(1)} all-to-all(bf16[32,2,1152]{2,1,0:T(2,128)(2,1)S(1)} %shard_map.123), channel_id=1, replica_groups={{0,1,2,3,4,5,6,7,8,9,10,11,12,13,14,15,16,17,18,19,20,21,22,23,24,25,26..., dimensions={0} | all-to-all | bytes 294912 | tf_op jit(solution)/shard_map/all_to_all | solution.py:488
  72.5 0.8 shard_map.124
  73.2 28.0 %all_to_all.21.got = bf16[16,2,1152]{2,1,0:T(2,128)(2,1)S(1)} all-to-all(bf16[16,2,1152]{2,1,0:T(2,128)(2,1)S(1)} %get-tuple-element.28), channel_id=1, replica_groups={{0,32,64,96,128,160,192,224,256,288,320,352,384,416,448,480},{16,48,80,..., dimensions={0} | all-to-all | bytes 147456 | tf_op jit(solution)/shard_map/all_to_all | solution.py:492
  101.3 13.1 %all_to_all.22.refs_0_ = bf16[32,2,1152]{2,1,0:T(2,128)(2,1)S(1)} all-to-all(bf16[32,2,1152]{2,1,0:T(2,128)(2,1)S(1)} %shard_map.125), channel_id=1, replica_groups={{0,1,2,3,4,5,6,7,8,9,10,11,12,13,14,15,16,17,18,19,20,21,22,23,24,25,26..., dimensions={0} | all-to-all | bytes 294912 | tf_op jit(solution)/shard_map/all_to_all | solution.py:494
  114.4 0.9 shard_map.126
  (11 shorter events, 0.1 us)
Async XLA Ops:
  0.6 40.1 %copy-start.1 = (bf16[32,16,3,3,3]{0,1,4,3,2:T(8,128)(2,1)S(1)}, bf16[32,16,3,3,3]{0,1,4,3,2:T(8,128)(2,1)}, u32[]{:S(2)}) copy-start(bf16[32,16,3,3,3]{0,1,4,3,2:T(8,128)(2,1)} %param.11) | copy-start | bytes 82948
  2.4 13.1 %collective-permute-start.3 = (bf16[11,32,128]{2,1,0:T(8,128)(2,1)}, bf16[11,32,128]{2,1,0:T(8,128)(2,1)S(1)}, u32[]{:S(2)}, u32[]{:S(2)}) collective-permute-start(bf16[11,32,128]{2,1,0:T(8,128)(2,1)} %shard_map.120.own), channel_id=1, source_target_pairs={{32,0},{48,16},{64,32},{80,48},{96,64},{112,80},{128,96},{144,112}... | collective-permute-start | bytes 270344 | tf_op jit(solution)/shard_map/ppermute | solution.py:427
  3.7 11.8 %collective-permute-start.2 = (bf16[11,32,128]{2,1,0:T(8,128)(2,1)}, bf16[11,32,128]{2,1,0:T(8,128)(2,1)S(1)}, u32[]{:S(2)}, u32[]{:S(2)}) collective-permute-start(bf16[11,32,128]{2,1,0:T(8,128)(2,1)} %shard_map.120.own), channel_id=1, source_target_pairs={{16,0},{32,16},{48,32},{64,48},{80,64},{96,80},{112,96},{128,112},... | collective-permute-start | bytes 270344 | tf_op jit(solution)/shard_map/ppermute | solution.py:427
  5.0 10.5 %collective-permute-start.1 = (bf16[11,32,128]{2,1,0:T(8,128)(2,1)}, bf16[11,32,128]{2,1,0:T(8,128)(2,1)S(1)}, u32[]{:S(2)}, u32[]{:S(2)}) collective-permute-start(bf16[11,32,128]{2,1,0:T(8,128)(2,1)} %shard_map.120.own), channel_id=1, source_target_pairs={{0,16},{16,32},{32,48},{48,64},{64,80},{80,96},{96,112},{112,128},... | collective-permute-start | bytes 270344 | tf_op jit(solution)/shard_map/ppermute | solution.py:426
  11.3 6.1 %collective-permute-start = (bf16[11,32,128]{2,1,0:T(8,128)(2,1)}, bf16[11,32,128]{2,1,0:T(8,128)(2,1)S(1)}, u32[]{:S(2)}, u32[]{:S(2)}) collective-permute-start(bf16[11,32,128]{2,1,0:T(8,128)(2,1)} %shard_map.120.own), channel_id=1, source_target_pairs={{0,32},{16,48},{32,64},{48,80},{64,96},{80,112},{96,128},{112,144}... | collective-permute-start | bytes 270344 | tf_op jit(solution)/shard_map/ppermute | solution.py:426
  17.4 0.9 copy-start
  18.3 22.5 %copy-start.3 = (bf16[2048,128]{1,0:T(8,128)(2,1)S(1)}, bf16[2048,128]{1,0:T(8,128)(2,1)}, u32[]{:S(2)}) copy-start(bf16[2048,128]{1,0:T(8,128)(2,1)} %constant.11.clone.refs_3_.refs_9_) | copy-start | bytes 1572868
  19.0 16.0 %collective-permute-start.5 = (bf16[38,32,128]{2,1,0:T(8,128)(2,1)S(1)}, bf16[38,32,128]{2,1,0:T(8,128)(2,1)S(1)}, u32[]{:S(2)}, u32[]{:S(2)}) collective-permute-start(bf16[38,32,128]{2,1,0:T(8,128)(2,1)S(1)} %get-tuple-element.18), channel_id=1, source_target_pairs={{1,0},{2,1},{3,2},{4,3},{5,4},{6,5},{7,6},{8,7},{9,8},{10,9},{11,1... | collective-permute-start | bytes 933896 | tf_op jit(solution)/shard_map/ppermute | solution.py:427
  28.5 6.6 %collective-permute-start.4 = (bf16[38,32,128]{2,1,0:T(8,128)(2,1)S(1)}, bf16[38,32,128]{2,1,0:T(8,128)(2,1)S(1)}, u32[]{:S(2)}, u32[]{:S(2)}) collective-permute-start(bf16[38,32,128]{2,1,0:T(8,128)(2,1)S(1)} %get-tuple-element.18), channel_id=1, source_target_pairs={{0,1},{1,2},{2,3},{3,4},{4,5},{5,6},{6,7},{7,8},{8,9},{9,10},{10,1... | collective-permute-start | bytes 933896 | tf_op jit(solution)/shard_map/ppermute | solution.py:426
  30.4 10.4 %all-to-all-start = ((bf16[16,40,128]{2,1,0:T(8,128)(2,1)}), bf16[16,40,128]{2,1,0:T(8,128)(2,1)S(1)}, u32[]{:S(2)}, u32[]{:S(2)}) async-start(bf16[16,40,128]{2,1,0:T(8,128)(2,1)} %get-tuple-element.19), calls=%async_computation | async-start | bytes 327680 | tf_op jit(solution)/shard_map/all_to_all | solution.py:459
  40.8 11.4 %copy-start.2 = (bf16[256,2304]{1,0:T(8,128)(2,1)S(1)}, bf16[256,2304]{1,0:T(8,128)(2,1)}, u32[]{:S(2)}) copy-start(bf16[256,2304]{1,0:T(8,128)(2,1)} %constant.12.clone.refs_10_) | copy-start | bytes 3538948
  40.8 11.4 %copy-start.4 = (bf16[256,512]{1,0:T(8,128)(2,1)S(1)}, bf16[256,512]{1,0:T(8,128)(2,1)}, u32[]{:S(2)}) copy-start(bf16[256,512]{1,0:T(8,128)(2,1)} %constant.14.clone.refs_12_) | copy-start | bytes 786436
  45.3 5.6 %collective-permute-start.7 = (bf16[8,32,128]{2,1,0:T(8,128)(2,1)S(1)}, bf16[8,32,128]{2,1,0:T(8,128)(2,1)S(1)}, u32[]{:S(2)}, u32[]{:S(2)}) collective-permute-start(bf16[8,32,128]{2,1,0:T(8,128)(2,1)S(1)} %get-tuple-element.21.refs_1_), channel_id=1, source_target_pairs={{1,0},{2,1},{3,2},{4,3},{5,4},{6,5},{7,6},{8,7},{9,8},{10,9},{11,1... | collective-permute-start | bytes 196616 | tf_op jit(solution)/shard_map/ppermute | solution.py:427
  47.7 4.6 %collective-permute-start.6 = (bf16[8,32,128]{2,1,0:T(8,128)(2,1)S(1)}, bf16[8,32,128]{2,1,0:T(8,128)(2,1)S(1)}, u32[]{:S(2)}, u32[]{:S(2)}) collective-permute-start(bf16[8,32,128]{2,1,0:T(8,128)(2,1)S(1)} %get-tuple-element.21.refs_1_), channel_id=1, source_target_pairs={{0,1},{1,2},{2,3},{3,4},{4,5},{5,6},{6,7},{7,8},{8,9},{9,10},{10,1... | collective-permute-start | bytes 196616 | tf_op jit(solution)/shard_map/ppermute | solution.py:426

commit v4 on v3

--- a/solution.py
+++ b/solution.py
@@ -162,8 +162,38 @@
     sent[...] = held[...].astype(BF16)
 
 
+def forward_weights(w_first, w_second, taps, w_a, w_b):
+    turned_w = dot_t(unit(16, BF16), w_first[...]).astype(BF16)
+    w_a[...] = jnp.concatenate(
+        [dot_t(turned_w, taps[256 * p : 256 * p + 256]).astype(BF16) for p in range(8)], axis=0
+    )
+    w_b[...] = dot_t(unit(32, BF16), w_second[...]).astype(BF16)
+
+
+def backward_weights(got, w_second, w_c, spreads, back_c, back_b, w_third, grads, flip_c, flip_b):
+    arrived = got[...].astype(F32)
+    for s in range(16):
+        for g in range(7):
+            w_third[4 * s : 4 * s + 4, 128 * g : 128 * g + 128] = arrived[s, 4 * g : 4 * g + 4]
+        for j in range(3):
+            grads[j, 4 * s : 4 * s + 4] = arrived[s, 28 + 4 * j : 32 + 4 * j]
+    w_c[...] = w_third[...].astype(BF16)
+    spread_c = feature_spread()
+    for j in range(3):
+        spreads[j] = dot(grads[j].astype(BF16), spread_c)
+    for j in range(27):
+        k = 26 - j
+        flip_c[64 * j : 64 * j + 64, :] = w_third[:, 32 * k : 32 * k + 32]
+    back_c[...] = dot_t(unit(32, BF16), flip_c[...].astype(BF16)).astype(BF16)
+    wb = w_second[...].astype(F32)
+    for j in range(27):
+        k = 26 - j
+        flip_b[:, 32 * j : 32 * j + 32] = wb[16 * k : 16 * k + 16]
+    back_b[...] = flip_b[...][:, 0:864].astype(BF16)
+
+
 def forward(
-    n_sx, field, w_first, w_second, taps,
+    n_sx, field, w_a, w_b,
     second, mask_a, patch_a, mask_b, patch_b, cells, rows_b, cols,
 ):
     ix, iy = lax.axis_index("sx"), lax.axis_index("sy")
@@ -176,11 +206,6 @@
             for d in range(38):
                 part = wide[96 * d : 96 * d + 96, 128 * t : 128 * t + 128]
                 cells[2 * half + t, d] = jnp.where(left, part[0:80], part[8:88]).astype(BF16)
-    turned_w = dot_t(unit(16, BF16), w_first[...]).astype(BF16)
-    w_a = jnp.concatenate(
-        [dot_t(turned_w, taps[256 * p : 256 * p + 256]).astype(BF16) for p in range(8)], axis=0
-    )
-    w_b = dot_t(unit(32, BF16), w_second[...]).astype(BF16)
     pair = lanes(128) // 64
     for two in range(9):
         rows = []
@@ -192,7 +217,7 @@
                         pieces.append(cells[t, 2 * d + kd, 16 * a : 16 * a + 16])
                 rows.append(jnp.concatenate(pieces, axis=1))
         patch = jnp.concatenate(rows, axis=0)
-        pre = dot(w_a, patch)
+        pre = dot(w_a[...], patch)
         act = leaky(pre)
         pool = act[0:16]
         for p in range(1, 8):
@@ -237,7 +262,7 @@
     for e in range(8):
         act = jnp.zeros((32, 512), F32)
         for d in (2 * e, 2 * e + 1):
-            pre = dot(w_b, cols[d : d + 3].reshape(432, 512))
+            pre = dot(w_b[...], cols[d : d + 3].reshape(432, 512))
             if 4 <= d < 12:
                 mask_b[d - 4] = jnp.where(pre > 0, 1.0, 0.0).astype(BF16)
             act = act + leaky(pre)
@@ -251,19 +276,11 @@
 
 
 def backward(
-    n_sx, prev, own, nxt, got, mask_a, patch_a, mask_b, patch_b, w_second, taps,
+    n_sx, prev, own, nxt, w_c, spreads, back_c, back_b, mask_a, patch_a, mask_b, patch_b, taps,
     shift_c, shift_d, spread_b,
-    parts, w_third, grads, cols_c, grads_c, cols_g, flip_c, flip_b, grads_b, cols_h, held,
+    parts, cols_c, grads_c, cols_g, grads_b, cols_h, held,
 ):
     ix, iy = lax.axis_index("sx"), lax.axis_index("sy")
-    arrived = got[...].astype(F32)
-    for s in range(16):
-        for g in range(7):
-            w_third[4 * s : 4 * s + 4, 128 * g : 128 * g + 128] = arrived[s, 4 * g : 4 * g + 4]
-        for j in range(3):
-            grads[j, 4 * s : 4 * s + 4] = arrived[s, 28 + 4 * j : 32 + 4 * j]
-    wide_w = w_third[...].astype(BF16)
-    w_c = wide_w[:, 0:864]
     tall = jnp.concatenate([prev[...], own[...], nxt[...]], axis=2).reshape(256, 384)
     joined = dot(tall, brick_join()).astype(BF16)
     for k in range(9):
@@ -272,13 +289,11 @@
             cols_c[d, 32 * k : 32 * k + 32] = shifted[32 * d : 32 * d + 32]
     row = lanes(256) // 32
     mine = jnp.logical_and(row >= 3, row < 5)
-    spread_c = feature_spread()
-    spreads = [dot(grads[j].astype(BF16), spread_c) for j in range(3)]
     pooled = jnp.zeros((64, 256), F32)
     third_wg = jnp.zeros((64, 864), F32)
     for e in range(1, 7):
         window = cols_c[e - 1 : e + 2].reshape(864, 256)
-        pre = dot(w_c, window)
+        pre = dot(w_c[:, 0:864], window)
         back = (jnp.where(pre > 0, 1.0, SLOPE) * spreads[(e - 1) // 2]).astype(BF16)
         grads_c[e - 1] = back
         if e in (3, 4):
@@ -290,11 +305,7 @@
         shifted = shifted.astype(BF16)
         for e in range(6):
             cols_g[e, 64 * k : 64 * k + 64] = shifted[64 * e : 64 * e + 64]
-    for j in range(27):
-        k = 26 - j
-        flip_c[64 * j : 64 * j + 64, :] = w_third[:, 32 * k : 32 * k + 32]
-    back_c = dot_t(unit(32, BF16), flip_c[...].astype(BF16)).astype(BF16)
-    ups = [dot(back_c, cols_g[e : e + 3].reshape(1728, 256)) for e in range(4)]
+    ups = [dot(back_c[...], cols_g[e : e + 3].reshape(1728, 256)) for e in range(4)]
     fine = dot_two(jnp.concatenate(ups, axis=0), spread_b[...])
     row = 4 * iy - 2 + lanes(512) // 64
     in_rows = jnp.logical_and(row >= 0, row < 64)
@@ -315,12 +326,7 @@
         shifted = shifted.astype(BF16)
         for d in range(6):
             cols_h[d, 32 * k : 32 * k + 32] = shifted[32 * d : 32 * d + 32]
-    wb = w_second[...].astype(F32)
-    for j in range(27):
-        k = 26 - j
-        flip_b[:, 32 * j : 32 * j + 32] = wb[16 * k : 16 * k + 16]
-    back_b = flip_b[...][:, 0:864].astype(BF16)
-    ups = [dot(back_b, cols_h[d : d + 3].reshape(864, 256)) for d in range(4)]
+    ups = [dot(back_b[...], cols_h[d : d + 3].reshape(864, 256)) for d in range(4)]
     left = lanes(128) < 64
     blocks = jnp.zeros((128, 256), F32)
     for d in range(4):
@@ -460,6 +466,10 @@
     prev, nxt = exchanged(tall, tall, "sy")
     field = jnp.concatenate([prev[:, 4:], tall, nxt, nxt[:, :4]], axis=1)
     field, got = lax.optimization_barrier((field, got))
+    w_a, w_b = call(
+        forward_weights,
+        [((128, 256), BF16), ((32, 432), BF16)], [], first_w, second_w, taps, cost=5e8,
+    )
     second, mask_a, patch_a, mask_b, patch_b = call(
         lambda *refs: forward(n_sx, *refs),
         [
@@ -467,18 +477,24 @@
             ((8, 32, 512), BF16), ((6, 144, 512), BF16),
         ],
         [((4, 38, 80, 128), BF16), ((18, 144, 128), BF16), ((18, 144, 512), BF16)],
-        field, first_w, second_w, taps, cost=5e9,
+        field, w_a, w_b, cost=5e9,
     )
     prev, nxt = exchanged(second, second, "sy")
+    w_c, spreads, back_c, back_b = call(
+        backward_weights,
+        [((64, 896), BF16), ((3, 64, 256), F32), ((32, 1728), BF16), ((16, 864), BF16)],
+        [((64, 896), F32), ((3, 64, 128), F32), ((1728, 32), F32), ((16, 896), F32)],
+        got, second_w, cost=15e8,
+    )
     (parts,) = call(
         lambda *refs: backward(n_sx, *refs),
         [((32, 2, 1152), BF16)],
         [
-            ((64, 896), F32), ((3, 64, 128), F32), ((8, 288, 256), BF16), ((6, 64, 256), BF16),
-            ((6, 576, 256), BF16), ((1728, 32), F32), ((16, 896), F32),
+            ((8, 288, 256), BF16), ((6, 64, 256), BF16),
+            ((6, 576, 256), BF16),
             ((6, 32, 512), BF16), ((6, 288, 256), BF16), ((32, 2, 1152), F32),
         ],
-        prev, second, nxt, got, mask_a, patch_a, mask_b, patch_b, second_w, taps,
+        prev, second, nxt, w_c, spreads, back_c, back_b, mask_a, patch_a, mask_b, patch_b, taps,
         table(tap_shift(8, 32, 0, 8)), table(tap_shift(8, 64, 2, 4)),
         table(second_spread()), cost=11e9,
     )

time: 116 us -> 116 us (level)
  starting transfers between devices: 33.9 us -> 28.3 us
  waiting for transfers between devices: 8.38 us -> 13.5 us
  local copies, waits for them, and re-layouts: 1.8 us -> 3.74 us
  blocking collectives: 54.8 us -> 52.9 us
    ppermute x4, waiting for transfers between devices: 0.01 us -> 9.89 us  [exchanged(): lax.ppermute(to_prev, axis, [(i + step, i) for i in range(ends)])]
    ppermute x4, starting transfers between devices: 14.4 us -> 8.06 us  [exchanged(): lax.ppermute(to_prev, axis, [(i + step, i) for i in range(ends)])]
    ppermute x4, waiting for transfers between devices: 3.13 us -> 0.01 us  [exchanged(): lax.ppermute(to_next, axis, [(i, i + step) for i in range(ends)])]
    unnamed x10 -> x14, local copies, waits for them, and re-layouts: 0.9 us -> 2.84 us
    all_to_all x1, blocking collectives: 28 us -> 26.3 us  [shards(): got = lax.all_to_all(total, 'sx', 0, 0, tiled=True, axis_index_groups=lines)]
    all_to_all x1, waiting for transfers between devices: 5.24 us -> 3.62 us  [shards(): got = lax.all_to_all(sent, 'sy', 0, 0, tiled=True)]
    all_to_all x1, starting transfers between devices: 3.83 us -> 5.25 us  [shards(): got = lax.all_to_all(sent, 'sy', 0, 0, tiled=True)]
    pallas_call x7 -> x9, Pallas kernels: 15.3 us -> 15.8 us  [call(): pl.pallas_call(body, out_shape=[jax.ShapeDtypeStruct(shape, dtype) for sh...]
  transfers between devices with their start and end apart: 9 -> 9, of which waited for: 3 -> 4; matrix products, arithmetic and copies ran while one was open for 1% -> 1% of each run, Pallas kernels for 0% -> 1%
where the time goes in v4:
time: 116 us; the launch traced here: 115 us
  blocking collectives  52.9 us (46%)
  starting transfers between devices  28.3 us (24%)
  Pallas kernels  15.8 us (14%)
  waiting for transfers between devices  13.5 us (12%)
  local copies, waits for them, and re-layouts  3.74 us (3%)
    all_to_all x1, blocking collectives, shards(): got = lax.all_to_all(total, 'sx', 0, 0, tiled=True, axis_index_groups=lines)  26.3 us
    pallas_call x9, Pallas kernels, call(): pl.pallas_call(body, out_shape=[jax.ShapeDtypeStruct(shape, dtype) for sh...  15.8 us
    ppermute x4, starting transfers between devices, exchanged(): lax.ppermute(to_next, axis, [(i, i + step) for i in range(ends)])  15 us
    all_to_all x1, blocking collectives, shards(): lax.all_to_all(parts, both, 0, 0, tiled=True, axis_index_groups=planes)  13.5 us
    all_to_all x1, blocking collectives, shards(): lax.all_to_all(total, both, 0, 0, tiled=True, axis_index_groups=planes)  13.1 us
    ppermute x4, waiting for transfers between devices, exchanged(): lax.ppermute(to_prev, axis, [(i + step, i) for i in range(ends)])  9.89 us
    ppermute x4, starting transfers between devices, exchanged(): lax.ppermute(to_prev, axis, [(i + step, i) for i in range(ends)])  8.06 us
    all_to_all x1, starting transfers between devices, shards(): got = lax.all_to_all(sent, 'sy', 0, 0, tiled=True)  5.25 us
  transfers between devices with their start and end apart: 9, of which 4 were waited for; matrix products, arithmetic and copies ran while one was open for 1% of the time, Pallas kernels for 1%

profile of v4, /device:TPU:1, one launch (start us, length us, event | category | flops | bytes accessed | tf_op | source)
XLA Modules:
  0.0 115.4 jit_solution(1566936862919729859)
XLA Ops:
  0.6 1.8 %shard_map.120.own = bf16[11,32,128]{2,1,0:T(8,128)(2,1)} custom-call(bf16[4,8,8,128]{3,2,1,0:T(8,128)(2,1)} %volume_in.1, bf16[4,16,16]{2,1,0:T(8,128)(2,1)} %bitcast.24, bf16[27,4,32]{2,1,0:T(4,128)(2,1)} %bitcast.23), custom_call_target="tpu_custom_call" | custom-call | flops 100000000 | bytes 100000 | tf_op jit(solution)/shard_map/pallas_call | solution.py:419
  2.4 4.4 %collective-permute-start = (bf16[11,32,128]{2,1,0:T(8,128)(2,1)}, bf16[11,32,128]{2,1,0:T(8,128)(2,1)S(1)}, u32[]{:S(2)}, u32[]{:S(2)}) collective-permute-start(bf16[11,32,128]{2,1,0:T(8,128)(2,1)} %shard_map.120.own), channel_id=1, source_target_pairs={{0,32},{16,48},{32,64},{48,80},{64,96},{80,112},{96,128},{112,144}... | collective-permute-start | bytes 270344 | tf_op jit(solution)/shard_map/ppermute | solution.py:432
  6.8 4.8 %collective-permute-start.1 = (bf16[11,32,128]{2,1,0:T(8,128)(2,1)}, bf16[11,32,128]{2,1,0:T(8,128)(2,1)S(1)}, u32[]{:S(2)}, u32[]{:S(2)}) collective-permute-start(bf16[11,32,128]{2,1,0:T(8,128)(2,1)} %shard_map.120.own), channel_id=1, source_target_pairs={{0,16},{16,32},{32,48},{48,64},{64,80},{80,96},{96,112},{112,128},... | collective-permute-start | bytes 270344 | tf_op jit(solution)/shard_map/ppermute | solution.py:432
  11.6 1.3 %collective-permute-start.2 = (bf16[11,32,128]{2,1,0:T(8,128)(2,1)}, bf16[11,32,128]{2,1,0:T(8,128)(2,1)S(1)}, u32[]{:S(2)}, u32[]{:S(2)}) collective-permute-start(bf16[11,32,128]{2,1,0:T(8,128)(2,1)} %shard_map.120.own), channel_id=1, source_target_pairs={{16,0},{32,16},{48,32},{64,48},{80,64},{96,80},{112,96},{128,112},... | collective-permute-start | bytes 270344 | tf_op jit(solution)/shard_map/ppermute | solution.py:433
  12.9 1.3 %collective-permute-start.3 = (bf16[11,32,128]{2,1,0:T(8,128)(2,1)}, bf16[11,32,128]{2,1,0:T(8,128)(2,1)S(1)}, u32[]{:S(2)}, u32[]{:S(2)}) collective-permute-start(bf16[11,32,128]{2,1,0:T(8,128)(2,1)} %shard_map.120.own), channel_id=1, source_target_pairs={{32,0},{48,16},{64,32},{80,48},{96,64},{112,80},{128,96},{144,112}... | collective-permute-start | bytes 270344 | tf_op jit(solution)/shard_map/ppermute | solution.py:433
  14.2 0.0 collective-permute-done.1.prev
  14.2 4.4 %collective-permute-done.2.nxt = bf16[11,32,128]{2,1,0:T(8,128)(2,1)S(1)} collective-permute-done((bf16[11,32,128]{2,1,0:T(8,128)(2,1)}, bf16[11,32,128]{2,1,0:T(8,128)(2,1)S(1)}, u32[]{:S(2)}, u32[]{:S(2)}) %collective-permute-start.2) | collective-permute-done | bytes 90144 | tf_op jit(solution)/shard_map/ppermute | solution.py:433
  18.6 2.3 %collective-permute-done.3.far_nxt = bf16[11,32,128]{2,1,0:T(8,128)(2,1)S(1)} collective-permute-done((bf16[11,32,128]{2,1,0:T(8,128)(2,1)}, bf16[11,32,128]{2,1,0:T(8,128)(2,1)S(1)}, u32[]{:S(2)}, u32[]{:S(2)}) %collective-permute-start.3) | collective-permute-done | bytes 90144 | tf_op jit(solution)/shard_map/ppermute | solution.py:433
  20.9 0.9 copy-done
  21.8 0.7 shard_map.121
  22.5 3.6 %collective-permute-start.5 = (bf16[38,32,128]{2,1,0:T(8,128)(2,1)S(1)}, bf16[38,32,128]{2,1,0:T(8,128)(2,1)S(1)}, u32[]{:S(2)}, u32[]{:S(2)}) collective-permute-start(bf16[38,32,128]{2,1,0:T(8,128)(2,1)S(1)} %get-tuple-element.24), channel_id=1, source_target_pairs={{1,0},{2,1},{3,2},{4,3},{5,4},{6,5},{7,6},{8,7},{9,8},{10,9},{11,1... | collective-permute-start | bytes 933896 | tf_op jit(solution)/shard_map/ppermute | solution.py:433
  26.0 3.1 %collective-permute-start.4 = (bf16[38,32,128]{2,1,0:T(8,128)(2,1)S(1)}, bf16[38,32,128]{2,1,0:T(8,128)(2,1)S(1)}, u32[]{:S(2)}, u32[]{:S(2)}) collective-permute-start(bf16[38,32,128]{2,1,0:T(8,128)(2,1)S(1)} %get-tuple-element.24), channel_id=1, source_target_pairs={{0,1},{1,2},{2,3},{3,4},{4,5},{5,6},{6,7},{7,8},{8,9},{9,10},{10,1... | collective-permute-start | bytes 933896 | tf_op jit(solution)/shard_map/ppermute | solution.py:432
  29.1 0.8 reshape.34
  29.9 5.2 %all-to-all-start = ((bf16[16,40,128]{2,1,0:T(8,128)(2,1)}), bf16[16,40,128]{2,1,0:T(8,128)(2,1)S(1)}, u32[]{:S(2)}, u32[]{:S(2)}) async-start(bf16[16,40,128]{2,1,0:T(8,128)(2,1)} %get-tuple-element.25), calls=%async_computation | async-start | bytes 327680 | tf_op jit(solution)/shard_map/all_to_all | solution.py:465
  35.2 0.9 copy-done.1
  36.1 1.0 copy-done.4
  37.1 0.4 shard_map.122
  37.6 0.1 slice.8
  37.7 0.4 pad_maximum_fusion.refs_0_
  38.1 3.6 %all-to-all-done.got = bf16[16,40,128]{2,1,0:T(8,128)(2,1)S(1)} async-done(((bf16[16,40,128]{2,1,0:T(8,128)(2,1)}), bf16[16,40,128]{2,1,0:T(8,128)(2,1)S(1)}, u32[]{:S(2)}, u32[]{:S(2)}) %all-to-all-start) | async-done | bytes 163872 | tf_op jit(solution)/shard_map/all_to_all | solution.py:465
  41.7 4.2 %shard_map.123 = (bf16[8,32,128]{2,1,0:T(8,128)(2,1)S(1)}, bf16[4,128,384]{2,1,0:T(8,128)(2,1)S(1)}, bf16[4,256,384]{2,1,0:T(8,128)(2,1)S(1)}, bf16[8,32,512]{2,1,0:T(8,128)(2,1)S(1)}, bf16[6,144,512]{2,1,0:T(8,128)(2,1)S(1)}) custom-call(bf16[38,96,128]{2,1,0:T(8,128)(2,1)S(1)} %pad_maximum_fusion.refs_0_, bf16[128,256]{1,0:T(8,128)(2,1)S(1)} %get-tuple-element.27.refs_1_, ...), custom_call_target="tpu_custom_call" | custom-call | flops 5000000000 | bytes 100000 | tf_op jit(solution)/shard_map/pallas_call | solution.py:419
  45.9 0.0 copy-start.6
  45.9 2.7 %collective-permute-start.6 = (bf16[8,32,128]{2,1,0:T(8,128)(2,1)S(1)}, bf16[8,32,128]{2,1,0:T(8,128)(2,1)S(1)}, u32[]{:S(2)}, u32[]{:S(2)}) collective-permute-start(bf16[8,32,128]{2,1,0:T(8,128)(2,1)S(1)} %get-tuple-element.29.refs_1_), channel_id=1, source_target_pairs={{0,1},{1,2},{2,3},{3,4},{4,5},{5,6},{6,7},{7,8},{8,9},{9,10},{10,1... | collective-permute-start | bytes 196616 | tf_op jit(solution)/shard_map/ppermute | solution.py:432
  48.6 1.9 %collective-permute-start.7 = (bf16[8,32,128]{2,1,0:T(8,128)(2,1)S(1)}, bf16[8,32,128]{2,1,0:T(8,128)(2,1)S(1)}, u32[]{:S(2)}, u32[]{:S(2)}) collective-permute-start(bf16[8,32,128]{2,1,0:T(8,128)(2,1)S(1)} %get-tuple-element.29.refs_1_), channel_id=1, source_target_pairs={{1,0},{2,1},{3,2},{4,3},{5,4},{6,5},{7,6},{8,7},{9,8},{10,9},{11,1... | collective-permute-start | bytes 196616 | tf_op jit(solution)/shard_map/ppermute | solution.py:433
  50.6 0.4 shard_map.124
  51.0 3.2 %collective-permute-done.7.refs_2_ = bf16[8,32,128]{2,1,0:T(8,128)(2,1)S(1)} collective-permute-done((bf16[8,32,128]{2,1,0:T(8,128)(2,1)S(1)}, bf16[8,32,128]{2,1,0:T(8,128)(2,1)S(1)}, u32[]{:S(2)}, u32[]{:S(2)}) %collective-permute-start.7) | collective-permute-done | bytes 65568 | tf_op jit(solution)/shard_map/ppermute | solution.py:433
  54.2 6.6 %shard_map.125 = bf16[32,2,1152]{2,1,0:T(2,128)(2,1)S(1)} custom-call(bf16[8,32,128]{2,1,0:T(8,128)(2,1)S(1)} %collective-permute-done.6.refs_0_, bf16[8,32,128]{2,1,0:T(8,128)(2,1)S(1)} %get-tuple-element.29.refs_1_, bf16[8,32,128]{2,1,0:T(8,128)(2,1)S(1)} %collective-permute-done.7.refs_2_, bf16[64,896]{1,0:T(8,128)(2,1)S(1)} %get-tuple-element.31.refs_3_, ...), custom_call_target="tpu_custom_call" | custom-call | flops 11000000512 | bytes 100000 | tf_op jit(solution)/shard_map/pallas_call | solution.py:419
  60.8 13.5 %all_to_all.20.got = bf16[32,2,1152]{2,1,0:T(2,128)(2,1)S(1)} all-to-all(bf16[32,2,1152]{2,1,0:T(2,128)(2,1)S(1)} %shard_map.125), channel_id=1, replica_groups={{0,1,2,3,4,5,6,7,8,9,10,11,12,13,14,15,16,17,18,19,20,21,22,23,24,25,26..., dimensions={0} | all-to-all | bytes 294912 | tf_op jit(solution)/shard_map/all_to_all | solution.py:504
  74.3 0.8 shard_map.126
  75.0 26.3 %all_to_all.21.got = bf16[16,2,1152]{2,1,0:T(2,128)(2,1)S(1)} all-to-all(bf16[16,2,1152]{2,1,0:T(2,128)(2,1)S(1)} %get-tuple-element.40), channel_id=1, replica_groups={{0,32,64,96,128,160,192,224,256,288,320,352,384,416,448,480},{16,48,80,..., dimensions={0} | all-to-all | bytes 147456 | tf_op jit(solution)/shard_map/all_to_all | solution.py:508
  101.4 13.1 %all_to_all.22.refs_0_ = bf16[32,2,1152]{2,1,0:T(2,128)(2,1)S(1)} all-to-all(bf16[32,2,1152]{2,1,0:T(2,128)(2,1)S(1)} %shard_map.127), channel_id=1, replica_groups={{0,1,2,3,4,5,6,7,8,9,10,11,12,13,14,15,16,17,18,19,20,21,22,23,24,25,26..., dimensions={0} | all-to-all | bytes 294912 | tf_op jit(solution)/shard_map/all_to_all | solution.py:510
  114.5 0.9 shard_map.128
  (17 shorter events, 0.1 us)
Async XLA Ops:
  2.4 11.8 %collective-permute-start = (bf16[11,32,128]{2,1,0:T(8,128)(2,1)}, bf16[11,32,128]{2,1,0:T(8,128)(2,1)S(1)}, u32[]{:S(2)}, u32[]{:S(2)}) collective-permute-start(bf16[11,32,128]{2,1,0:T(8,128)(2,1)} %shard_map.120.own), channel_id=1, source_target_pairs={{0,32},{16,48},{32,64},{48,80},{64,96},{80,112},{96,128},{112,144}... | collective-permute-start | bytes 270344 | tf_op jit(solution)/shard_map/ppermute | solution.py:432
  6.8 7.4 %collective-permute-start.1 = (bf16[11,32,128]{2,1,0:T(8,128)(2,1)}, bf16[11,32,128]{2,1,0:T(8,128)(2,1)S(1)}, u32[]{:S(2)}, u32[]{:S(2)}) collective-permute-start(bf16[11,32,128]{2,1,0:T(8,128)(2,1)} %shard_map.120.own), channel_id=1, source_target_pairs={{0,16},{16,32},{32,48},{48,64},{64,80},{80,96},{96,112},{112,128},... | collective-permute-start | bytes 270344 | tf_op jit(solution)/shard_map/ppermute | solution.py:432
  11.6 7.0 %collective-permute-start.2 = (bf16[11,32,128]{2,1,0:T(8,128)(2,1)}, bf16[11,32,128]{2,1,0:T(8,128)(2,1)S(1)}, u32[]{:S(2)}, u32[]{:S(2)}) collective-permute-start(bf16[11,32,128]{2,1,0:T(8,128)(2,1)} %shard_map.120.own), channel_id=1, source_target_pairs={{16,0},{32,16},{48,32},{64,48},{80,64},{96,80},{112,96},{128,112},... | collective-permute-start | bytes 270344 | tf_op jit(solution)/shard_map/ppermute | solution.py:433
  12.9 8.0 %collective-permute-start.3 = (bf16[11,32,128]{2,1,0:T(8,128)(2,1)}, bf16[11,32,128]{2,1,0:T(8,128)(2,1)S(1)}, u32[]{:S(2)}, u32[]{:S(2)}) collective-permute-start(bf16[11,32,128]{2,1,0:T(8,128)(2,1)} %shard_map.120.own), channel_id=1, source_target_pairs={{32,0},{48,16},{64,32},{80,48},{96,64},{112,80},{128,96},{144,112}... | collective-permute-start | bytes 270344 | tf_op jit(solution)/shard_map/ppermute | solution.py:433
  20.9 0.9 copy-start
  22.5 15.1 %collective-permute-start.5 = (bf16[38,32,128]{2,1,0:T(8,128)(2,1)S(1)}, bf16[38,32,128]{2,1,0:T(8,128)(2,1)S(1)}, u32[]{:S(2)}, u32[]{:S(2)}) collective-permute-start(bf16[38,32,128]{2,1,0:T(8,128)(2,1)S(1)} %get-tuple-element.24), channel_id=1, source_target_pairs={{1,0},{2,1},{3,2},{4,3},{5,4},{6,5},{7,6},{8,7},{9,8},{10,9},{11,1... | collective-permute-start | bytes 933896 | tf_op jit(solution)/shard_map/ppermute | solution.py:433
  26.0 11.5 %collective-permute-start.4 = (bf16[38,32,128]{2,1,0:T(8,128)(2,1)S(1)}, bf16[38,32,128]{2,1,0:T(8,128)(2,1)S(1)}, u32[]{:S(2)}, u32[]{:S(2)}) collective-permute-start(bf16[38,32,128]{2,1,0:T(8,128)(2,1)S(1)} %get-tuple-element.24), channel_id=1, source_target_pairs={{0,1},{1,2},{2,3},{3,4},{4,5},{5,6},{6,7},{7,8},{8,9},{9,10},{10,1... | collective-permute-start | bytes 933896 | tf_op jit(solution)/shard_map/ppermute | solution.py:432
  29.9 11.7 %all-to-all-start = ((bf16[16,40,128]{2,1,0:T(8,128)(2,1)}), bf16[16,40,128]{2,1,0:T(8,128)(2,1)S(1)}, u32[]{:S(2)}, u32[]{:S(2)}) async-start(bf16[16,40,128]{2,1,0:T(8,128)(2,1)} %get-tuple-element.25), calls=%async_computation | async-start | bytes 327680 | tf_op jit(solution)/shard_map/all_to_all | solution.py:465
  35.2 0.9 copy-start.1
  36.1 1.0 copy-start.4
  41.7 8.9 %copy-start.2 = (bf16[32,16,3,3,3]{0,1,4,3,2:T(8,128)(2,1)S(1)}, bf16[32,16,3,3,3]{0,1,4,3,2:T(8,128)(2,1)}, u32[]{:S(2)}) copy-start(bf16[32,16,3,3,3]{0,1,4,3,2:T(8,128)(2,1)} %param.11) | copy-start | bytes 82948
  45.9 8.3 %copy-start.3 = (bf16[256,2304]{1,0:T(8,128)(2,1)S(1)}, bf16[256,2304]{1,0:T(8,128)(2,1)}, u32[]{:S(2)}) copy-start(bf16[256,2304]{1,0:T(8,128)(2,1)} %constant.12.clone.refs_12_) | copy-start | bytes 3538948
  45.9 8.3 %copy-start.5 = (bf16[2048,128]{1,0:T(8,128)(2,1)S(1)}, bf16[2048,128]{1,0:T(8,128)(2,1)}, u32[]{:S(2)}) copy-start(bf16[2048,128]{1,0:T(8,128)(2,1)} %constant.11.clone.taps.refs_11_) | copy-start | bytes 1572868
  45.9 8.3 %copy-start.6 = (bf16[256,512]{1,0:T(8,128)(2,1)S(1)}, bf16[256,512]{1,0:T(8,128)(2,1)}, u32[]{:S(2)}) copy-start(bf16[256,512]{1,0:T(8,128)(2,1)} %constant.14.clone.refs_14_) | copy-start | bytes 786436
  45.9 5.0 %collective-permute-start.6 = (bf16[8,32,128]{2,1,0:T(8,128)(2,1)S(1)}, bf16[8,32,128]{2,1,0:T(8,128)(2,1)S(1)}, u32[]{:S(2)}, u32[]{:S(2)}) collective-permute-start(bf16[8,32,128]{2,1,0:T(8,128)(2,1)S(1)} %get-tuple-element.29.refs_1_), channel_id=1, source_target_pairs={{0,1},{1,2},{2,3},{3,4},{4,5},{5,6},{6,7},{7,8},{8,9},{9,10},{10,1... | collective-permute-start | bytes 196616 | tf_op jit(solution)/shard_map/ppermute | solution.py:432
  48.6 5.6 %collective-permute-start.7 = (bf16[8,32,128]{2,1,0:T(8,128)(2,1)S(1)}, bf16[8,32,128]{2,1,0:T(8,128)(2,1)S(1)}, u32[]{:S(2)}, u32[]{:S(2)}) collective-permute-start(bf16[8,32,128]{2,1,0:T(8,128)(2,1)S(1)} %get-tuple-element.29.refs_1_), channel_id=1, source_target_pairs={{1,0},{2,1},{3,2},{4,3},{5,4},{6,5},{7,6},{8,7},{9,8},{10,9},{11,1... | collective-permute-start | bytes 196616 | tf_op jit(solution)/shard_map/ppermute | solution.py:433
